TPU v7x, 32 devices: a whole 2x2x4 slice. The times are simulated.
32 devices in a mesh: ccd: 8 (over y, x, core), amp: 4 (over z).
Axes of the slice: x: 2, y: 2, z: 4, core: 2. Of those that a mesh axis runs over, the one named last changes fastest.
Arguments:
- science: float32 [8, 512, 4096], P('ccd', 'amp'), may hold values from -6 to 6
- patches: float32 [8, 4, 4, 256, 256], P('ccd', 'amp'), may hold values from -6 to 6
- coeffs: float32 [8, 40, 6], P('ccd'), may hold values from -0.9 to 0.9
- tile_owner: int32 [8, 4, 32, 1], replicated, may hold values from 0 to 7; in each aligned block of 32 rows (0 to 31, 32 to 63, ..., all dimensions but the last counted through in order) at most 8 rows name the same one
- tile_patch: int32 [8, 4, 32], replicated, may hold values from 0 to 3
- tile_offset: int32 [8, 4, 32, 2], replicated, may hold values from 0 to 128
Outputs:
- difference: float32 [8, 512, 4096], P('ccd', 'amp')
Inputs may be any that keep to these rules, and one draw needn't show every extreme that they name: `tile_owner`: among the 32 tiles of one strip, at most 8 name the same owner.
All inputs are finite; a program needn't handle non-finite values.
Results may differ from a plain program's by a relative error of at most 0.0031.
Values may be sent and summed in bfloat16 or wider, within the bound.
A program may use at most 128 MiB of HBM per device.

v0:
```python
import math

import jax
import jax.numpy as jnp
from jax import lax
from jax.sharding import PartitionSpec as P

TS = 128
HALF = 10


gauss_widths = (1.0, 2.0, 4.0)
poly_degrees = (4, 4, 3)


def with_halo(block, sides, width):
    for axis, dim in sides:
        count = lax.axis_size(axis)
        forward = [(i, i + 1) for i in range(count - 1)]
        backward = [(target, source) for source, target in forward]
        low = lax.ppermute(
            lax.slice_in_dim(block, block.shape[dim] - width, None, axis=dim), axis, forward
        )
        high = lax.ppermute(lax.slice_in_dim(block, 0, width, axis=dim), axis, backward)
        block = jnp.concatenate([low, block, high], axis=dim)
    return block


def factor_table(half):
    offsets = jnp.arange(-half, half + 1).astype(jnp.float32)
    shapes = []
    for sigma_px, degree in zip(gauss_widths, poly_degrees):
        for exponent in range(degree + 1):
            profile = (
                jnp.exp(-offsets * offsets / (2.0 * sigma_px * sigma_px))
                * (offsets / half) ** exponent
            )
            shapes.append(profile / jnp.sum(jnp.abs(profile)))
    return jnp.stack(shapes).astype(jnp.bfloat16)


def across_matrices(factors, half):
    column = jnp.arange(256)[:, None]
    output = jnp.arange(128)[None, :]
    lag_cols = column - 64 - output
    tap_offsets = jnp.arange(-half, half + 1)
    select = (lag_cols[:, :, None] == tap_offsets[None, None, :]).astype(jnp.float32)
    mats = jnp.einsum(
        "cqt,ht->hcq", select, factors.astype(jnp.float32), precision=lax.Precision.HIGHEST
    )
    return mats.astype(jnp.bfloat16)


def down_matrices(factors, half, strip_rows):
    target = jnp.arange(strip_rows)[:, None]
    source = jnp.arange(strip_rows + 2 * half)[None, :]
    lag_rows = source - half - target
    tap_offsets = jnp.arange(-half, half + 1)
    select = (lag_rows[:, :, None] == tap_offsets[None, None, :]).astype(jnp.float32)
    mats = jnp.einsum(
        "yrt,ht->hyr", select, factors.astype(jnp.float32), precision=lax.Precision.HIGHEST
    )
    return mats.astype(jnp.bfloat16)


def strip_model(padded, coeff_rows, row_first, total_rows, across_mats, down_mats):
    padded_rows, columns = padded.shape
    strip_rows = padded_rows - 2 * HALF
    block_count = columns // 128
    blocks = padded.reshape(padded_rows, block_count, 128)
    zero_block = jnp.zeros((padded_rows, 1, 128), padded.dtype)
    before = jnp.concatenate([zero_block, blocks[:, :-1]], axis=1)
    after = jnp.concatenate([blocks[:, 1:], zero_block], axis=1)
    factor_count = across_mats.shape[0]
    rim_zeros = jnp.zeros((factor_count, 64, 128), across_mats.dtype)
    left_mat = jnp.concatenate([rim_zeros, across_mats[:, :64]], axis=1)
    centre_mat = across_mats[:, 64:192]
    right_mat = jnp.concatenate([across_mats[:, 192:], rim_zeros], axis=1)
    per_group = math.gcd(block_count, 8)
    group_count = block_count // per_group
    group_cols = per_group * 128
    ycoord = (
        2.0 * (row_first + jnp.arange(strip_rows)).astype(jnp.float32) + 1.0
    ) / total_rows - 1.0

    def one_group(group_index, result):
        first_block = group_index * per_group
        own_part = lax.dynamic_slice_in_dim(blocks, first_block, per_group, 1)
        before_part = lax.dynamic_slice_in_dim(before, first_block, per_group, 1)
        after_part = lax.dynamic_slice_in_dim(after, first_block, per_group, 1)
        across_all = jnp.einsum(
            "rbc,hcq->hrbq", own_part, centre_mat, preferred_element_type=jnp.float32
        )
        across_all = across_all + jnp.einsum(
            "rbc,hcq->hrbq", before_part, left_mat, preferred_element_type=jnp.float32
        )
        across_all = across_all + jnp.einsum(
            "rbc,hcq->hrbq", after_part, right_mat, preferred_element_type=jnp.float32
        )
        across_all = across_all.astype(jnp.bfloat16).reshape(factor_count, padded_rows, group_cols)
        xcoord = (
            2.0 * (first_block * 128 + jnp.arange(group_cols)).astype(jnp.float32) + 1.0
        ) / columns - 1.0
        xgrid = jnp.broadcast_to(xcoord[None, :], (strip_rows, group_cols))
        ygrid = jnp.broadcast_to(ycoord[:, None], (strip_rows, group_cols))
        poly_terms = jnp.stack(
            [jnp.ones_like(xgrid), xgrid, ygrid, xgrid * xgrid, xgrid * ygrid, ygrid * ygrid]
        )
        psf_part = jnp.zeros((strip_rows, group_cols), jnp.float32)
        basis_first = 0
        first_factor = 0
        for degree in poly_degrees:
            for across_pow in range(degree + 1):
                count = degree + 1 - across_pow
                kernels = down_mats[first_factor : first_factor + count]
                convolved = jnp.einsum(
                    "kyr,rx->kyx",
                    kernels,
                    across_all[first_factor + across_pow],
                    preferred_element_type=jnp.float32,
                )
                weights = coeff_rows[basis_first : basis_first + count]
                folded = jnp.einsum(
                    "km,kyx->myx", weights, convolved, precision=lax.Precision.HIGHEST
                )
                psf_part = psf_part + jnp.sum(folded * poly_terms, axis=0)
                basis_first = basis_first + count
            first_factor = first_factor + degree + 1
        return lax.dynamic_update_slice_in_dim(
            result, psf_part.reshape(strip_rows, per_group, 128), first_block, 1
        )

    result = lax.fori_loop(
        0, group_count, one_group, jnp.zeros((strip_rows, block_count, 128), jnp.float32)
    )
    return result.reshape(strip_rows, columns)


def cut_from_piece(piece, owner_id, patch_id, row_shift, col_shift):
    zero_index = jnp.zeros((), jnp.int32)
    start = (owner_id, zero_index, patch_id, row_shift, col_shift)
    return lax.dynamic_slice(piece, start, (1, 1, 1, TS, TS))[0, 0, 0]


def per_device(science, patches, coeffs, tile_owner, tile_patch, tile_offset):
    ccd_id = lax.axis_index("ccd")
    amp_id = lax.axis_index("amp")
    strip_rows = science.shape[1]
    columns = science.shape[2]
    owners = tile_owner[..., 0]
    mine_owner = owners[ccd_id, amp_id]
    mine_patch = tile_patch[ccd_id, amp_id]
    mine_shift = tile_offset[ccd_id, amp_id]
    tile_count = mine_owner.shape[0]
    empty_tiles = jnp.zeros((tile_count, TS, TS), jnp.bfloat16)
    piece = lax.all_gather(patches.astype(jnp.bfloat16), "ccd", axis=0, tiled=True)
    first_owner = jnp.int32(0)
    piece_count = piece.shape[0]
    local_owner = jnp.clip(mine_owner, 0, piece_count - 1)
    cropped = jax.vmap(cut_from_piece, in_axes=(None, 0, 0, 0, 0))(
        piece, local_owner, mine_patch, mine_shift[:, 0], mine_shift[:, 1]
    )
    inside = (mine_owner >= first_owner) & (mine_owner < first_owner + piece_count)
    tile_stack = jnp.where(inside[:, None, None], cropped, empty_tiles)
    per_row = columns // TS
    template_strip = (
        tile_stack.reshape(strip_rows // TS, per_row, TS, TS)
        .transpose(0, 2, 1, 3)
        .reshape(strip_rows, columns)
    )
    padded = with_halo(template_strip, (("amp", 0),), HALF)
    factors = factor_table(HALF)
    across_mats = across_matrices(factors, HALF)
    down_mats = down_matrices(factors, HALF, strip_rows)
    psf_model = strip_model(
        padded,
        coeffs[0],
        amp_id * strip_rows,
        lax.axis_size("amp") * strip_rows,
        across_mats,
        down_mats,
    )
    return (science[0] - psf_model)[None]


def solution(mesh):
    placed = (
        P("ccd", "amp", None),
        P("ccd", "amp", None, None, None),
        P("ccd", None, None),
        P(),
        P(),
        P(),
    )
    return jax.shard_map(
        per_device, mesh=mesh, in_specs=placed, out_specs=P("ccd", "amp", None), check_vma=False
    )
```

profile of v0, /device:TPU:0, one launch (start us, length us, event | category | flops | bytes accessed | tf_op | source)
XLA Modules:
  0.0 856.5 jit_solution(13145338902217975768)
XLA Ops:
  28.9 19.8 %all-gather.2.cloned.1.call-done = bf16[8,1,4,256,256]{4,3,2,1,0:T(8,128)(2,1)} async-done(((bf16[1,1,4,256,256]{4,3,2,1,0:T(8,128)(2,1)}), bf16[8,1,4,256,256]{4,3,2,1,0:T(8,128)(2,1)}) %all-gather.2.cloned.1.call-update) | async-done | bytes 4194320 | tf_op jit(solution)/shard_map/all_gather | solution.py:156
  48.7 135.2 %while.18 = (s32[]{:T(128)}, bf16[8,1,4,256,256]{4,3,2,1,0:T(8,128)(2,1)}, s32[32,5]{0,1:T(8,128)S(1)}, bf16[32,1,1,1,128,128]{5,4,3,2,1,0:T(8,128)(2,1)S(1)}, s32[]{:T(128)}) while((s32[]{:T(128)}, bf16[8,1,4,256,256]{4,3,2,1,0:T(8,128)(2,1)}, s32[32,5]{0,1:T(8,128)S(1)}, bf16[32,1,1,1,128,128]{5,4,3,2,1,0:T(8,128)(2,1)S(1)}, s32[]{:T(128)}) %tuple.103), condition=%wide.while_cond, body=%wide.while_body.sunk | while | flops 2 | bytes 65693 | solution.py:142
  49.4 3.5 bitcast_dynamic-update-slice_fusion.2
  57.8 3.5 bitcast_dynamic-update-slice_fusion.2
  62.1 3.5 bitcast_dynamic-update-slice_fusion.2
  66.3 3.5 bitcast_dynamic-update-slice_fusion.2
  70.5 3.5 bitcast_dynamic-update-slice_fusion.2
  205.0 639.2 %while.19 = (s32[]{:T(128)}, f32[128,32,128]{2,1,0:T(8,128)}, bf16[148,32,128]{2,1,0:T(8,128)(2,1)S(1)}, bf16[14,128,128]{2,1,0:T(8,128)(2,1)S(1)}, bf16[148,32,...) while((s32[]{:T(128)}, f32[128,32,128]{2,1,0:T(8,128)}, ...), condition=%wide.region_29.30_spmd.clone.clone, body=%wide.region_14.29_spmd.clone.clone.sunk | while | flops 3561308160 | bytes 274131584 | solution.py:133
  220.0 10.6 %stack.53 = f32[6,128,1024]{2,0,1:T(8,128)} concatenate(f32[1,128,1024]{2,0,1:T(1,128)} %broadcast.977, f32[1,128,1024]{2,0,1:T(1,128)S(1)} %broadcast_in_dim.115, f32[1,128,1024]{2,0,1:T(1,128)S(1)} %broadcast_in_dim.116, f32[1,128,1024]{2,0,1:T(1,128)S(1)} %stack.51, f32[1,128,1024]{2,0,1:T(1,128)S(1)} %broadcast_multiply_fusion.2, f32[1,128,1024]{2,0,1:T(1,128)S(1)} %stack.52), dimensions={0} | concatenate | bytes 6291456 | tf_op jit(solution)/shard_map/while/body/eval_jaxpr/stack | solution.py:106
  230.8 7.9 fusion.227
  243.1 7.4 fusion.230
  254.8 7.4 fusion.233
  266.6 7.8 fusion.238
  278.5 7.4 fusion.229
  290.0 7.4 fusion.232
  301.4 7.5 fusion.236
  311.0 7.4 fusion.228
  319.5 7.4 fusion.231
  328.0 7.6 fusion.235
  339.9 9.3 %fusion.234 = f32[128,1024]{1,0:T(8,128)} fusion(f32[6,128,1024]{2,0,1:T(8,128)} %stack.53, f32[5,128,1024]{2,0,1:T(8,128)} %copy.122, f32[40,6]{0,1:T(8,128)S(1)} %get-tuple-element.666), kind=kOutput, calls=%fused_computation.23.clone.1 | convolution fusion | flops 48627712 | bytes 6292416 | tf_op jit(solution)/shard_map/while/body/eval_jaxpr/km,kyx->myx/dot_general | solution.py:123
  350.0 3.7 copy.125
  353.8 8.6 %fusion.237 = f32[128,1024]{1,0:T(8,128)S(1)} fusion(f32[6,128,1024]{2,0,1:T(8,128)} %stack.53, f32[5,128,1024]{2,0,1:T(8,128)} %copy.125, f32[40,6]{0,1:T(8,128)S(1)} %get-tuple-element.666), kind=kOutput, calls=%fused_computation.33.clone.1 | convolution fusion | flops 48627712 | bytes 6292416 | tf_op jit(solution)/shard_map/while/body/eval_jaxpr/km,kyx->myx/dot_general | solution.py:123
  379.6 10.5 %stack.53 = f32[6,128,1024]{2,0,1:T(8,128)} concatenate(f32[1,128,1024]{2,0,1:T(1,128)} %broadcast.977, f32[1,128,1024]{2,0,1:T(1,128)S(1)} %broadcast_in_dim.115, f32[1,128,1024]{2,0,1:T(1,128)S(1)} %broadcast_in_dim.116, f32[1,128,1024]{2,0,1:T(1,128)S(1)} %stack.51, f32[1,128,1024]{2,0,1:T(1,128)S(1)} %broadcast_multiply_fusion.2, f32[1,128,1024]{2,0,1:T(1,128)S(1)} %stack.52), dimensions={0} | concatenate | bytes 6291456 | tf_op jit(solution)/shard_map/while/body/eval_jaxpr/stack | solution.py:106
  390.3 7.9 fusion.227
  402.7 7.4 fusion.230
  414.4 7.4 fusion.233
  426.1 7.6 fusion.238
  437.8 7.4 fusion.229
  449.3 7.4 fusion.232
  460.7 7.8 fusion.236
  470.6 7.4 fusion.228
  479.1 7.4 fusion.231
  487.5 7.5 fusion.235
  499.4 9.3 %fusion.234 = f32[128,1024]{1,0:T(8,128)} fusion(f32[6,128,1024]{2,0,1:T(8,128)} %stack.53, f32[5,128,1024]{2,0,1:T(8,128)} %copy.122, f32[40,6]{0,1:T(8,128)S(1)} %get-tuple-element.666), kind=kOutput, calls=%fused_computation.23.clone.1 | convolution fusion | flops 48627712 | bytes 6292416 | tf_op jit(solution)/shard_map/while/body/eval_jaxpr/km,kyx->myx/dot_general | solution.py:123
  509.5 3.7 copy.125
  513.3 8.6 %fusion.237 = f32[128,1024]{1,0:T(8,128)S(1)} fusion(f32[6,128,1024]{2,0,1:T(8,128)} %stack.53, f32[5,128,1024]{2,0,1:T(8,128)} %copy.125, f32[40,6]{0,1:T(8,128)S(1)} %get-tuple-element.666), kind=kOutput, calls=%fused_computation.33.clone.1 | convolution fusion | flops 48627712 | bytes 6292416 | tf_op jit(solution)/shard_map/while/body/eval_jaxpr/km,kyx->myx/dot_general | solution.py:123
  538.9 10.8 %stack.53 = f32[6,128,1024]{2,0,1:T(8,128)} concatenate(f32[1,128,1024]{2,0,1:T(1,128)} %broadcast.977, f32[1,128,1024]{2,0,1:T(1,128)S(1)} %broadcast_in_dim.115, f32[1,128,1024]{2,0,1:T(1,128)S(1)} %broadcast_in_dim.116, f32[1,128,1024]{2,0,1:T(1,128)S(1)} %stack.51, f32[1,128,1024]{2,0,1:T(1,128)S(1)} %broadcast_multiply_fusion.2, f32[1,128,1024]{2,0,1:T(1,128)S(1)} %stack.52), dimensions={0} | concatenate | bytes 6291456 | tf_op jit(solution)/shard_map/while/body/eval_jaxpr/stack | solution.py:106
  549.9 7.9 fusion.227
  562.2 7.4 fusion.230
  574.0 7.4 fusion.233
  585.7 7.5 fusion.238
  597.3 7.4 fusion.229
  608.8 7.4 fusion.232
  620.2 7.6 fusion.236
  629.9 7.4 fusion.228
  638.4 7.4 fusion.231
  646.9 7.8 fusion.235
  658.9 9.3 %fusion.234 = f32[128,1024]{1,0:T(8,128)} fusion(f32[6,128,1024]{2,0,1:T(8,128)} %stack.53, f32[5,128,1024]{2,0,1:T(8,128)} %copy.122, f32[40,6]{0,1:T(8,128)S(1)} %get-tuple-element.666), kind=kOutput, calls=%fused_computation.23.clone.1 | convolution fusion | flops 48627712 | bytes 6292416 | tf_op jit(solution)/shard_map/while/body/eval_jaxpr/km,kyx->myx/dot_general | solution.py:123
  669.0 3.6 copy.125
  672.8 8.6 %fusion.237 = f32[128,1024]{1,0:T(8,128)S(1)} fusion(f32[6,128,1024]{2,0,1:T(8,128)} %stack.53, f32[5,128,1024]{2,0,1:T(8,128)} %copy.125, f32[40,6]{0,1:T(8,128)S(1)} %get-tuple-element.666), kind=kOutput, calls=%fused_computation.33.clone.1 | convolution fusion | flops 48627712 | bytes 6292416 | tf_op jit(solution)/shard_map/while/body/eval_jaxpr/km,kyx->myx/dot_general | solution.py:123
  698.3 10.6 %stack.53 = f32[6,128,1024]{2,0,1:T(8,128)} concatenate(f32[1,128,1024]{2,0,1:T(1,128)} %broadcast.977, f32[1,128,1024]{2,0,1:T(1,128)S(1)} %broadcast_in_dim.115, f32[1,128,1024]{2,0,1:T(1,128)S(1)} %broadcast_in_dim.116, f32[1,128,1024]{2,0,1:T(1,128)S(1)} %stack.51, f32[1,128,1024]{2,0,1:T(1,128)S(1)} %broadcast_multiply_fusion.2, f32[1,128,1024]{2,0,1:T(1,128)S(1)} %stack.52), dimensions={0} | concatenate | bytes 6291456 | tf_op jit(solution)/shard_map/while/body/eval_jaxpr/stack | solution.py:106
  709.1 7.9 fusion.227
  721.5 7.4 fusion.230
  733.2 7.4 fusion.233
  745.0 7.8 fusion.238
  756.9 7.4 fusion.229
  768.4 7.4 fusion.232
  779.8 7.5 fusion.236
  789.4 7.4 fusion.228
  797.9 7.4 fusion.231
  806.4 7.6 fusion.235
  818.3 9.3 %fusion.234 = f32[128,1024]{1,0:T(8,128)} fusion(f32[6,128,1024]{2,0,1:T(8,128)} %stack.53, f32[5,128,1024]{2,0,1:T(8,128)} %copy.122, f32[40,6]{0,1:T(8,128)S(1)} %get-tuple-element.666), kind=kOutput, calls=%fused_computation.23.clone.1 | convolution fusion | flops 48627712 | bytes 6292416 | tf_op jit(solution)/shard_map/while/body/eval_jaxpr/km,kyx->myx/dot_general | solution.py:123
  828.4 3.7 copy.125
  832.2 8.6 %fusion.237 = f32[128,1024]{1,0:T(8,128)S(1)} fusion(f32[6,128,1024]{2,0,1:T(8,128)} %stack.53, f32[5,128,1024]{2,0,1:T(8,128)} %copy.125, f32[40,6]{0,1:T(8,128)S(1)} %get-tuple-element.666), kind=kOutput, calls=%fused_computation.33.clone.1 | convolution fusion | flops 48627712 | bytes 6292416 | tf_op jit(solution)/shard_map/while/body/eval_jaxpr/km,kyx->myx/dot_general | solution.py:123
  (655 shorter events, 370.6 us)
Async XLA Ops:
  6.5 42.2 %all-gather.2.cloned.1.call-start = ((), (), s32[]{:S(2)}) async-start(), calls=%async_computation | async-start | bytes 4718592 | tf_op jit(solution)/shard_map/all_gather | solution.py:156
  28.9 163.5 %copy-start.32 = (bf16[14,256,128]{2,0,1:T(8,128)(2,1)}, bf16[14,256,128]{2,0,1:T(8,128)(2,1)S(1)}, u32[]{:S(2)}) copy-start(bf16[14,256,128]{2,0,1:T(8,128)(2,1)S(1)} %fusion.62) | copy-start | bytes 2752516
  185.6 8.4 collective-permute-start
  189.8 7.6 collective-permute-start.1
  230.8 7.9 copy-start.23
  339.9 9.3 %copy-start.15 = (bf16[1,148,8,128]{3,2,0,1:T(8,128)(2,1)S(1)}, bf16[1,148,8,128]{3,2,0,1:T(8,128)(2,1)}, u32[]{:S(2)}) copy-start(bf16[1,148,8,128]{3,2,0,1:T(8,128)(2,1)} %get-tuple-element.604) | copy-start | bytes 909316 | tf_op jit(solution)/shard_map/while
  353.7 8.7 %copy-start.2 = (f32[128,1024]{1,0:T(8,128)S(1)}, f32[128,1024]{1,0:T(8,128)}, u32[]{:S(2)}) copy-start(f32[128,1024]{1,0:T(8,128)} %fusion.230) | copy-start | bytes 1572868 | tf_op jit(solution)/shard_map/while
  353.7 8.7 %copy-start.3 = (f32[128,1024]{1,0:T(8,128)S(1)}, f32[128,1024]{1,0:T(8,128)}, u32[]{:S(2)}) copy-start(f32[128,1024]{1,0:T(8,128)} %fusion.233) | copy-start | bytes 1572868 | tf_op jit(solution)/shard_map/while
  353.7 8.7 %copy-start.4 = (f32[128,1024]{1,0:T(8,128)S(1)}, f32[128,1024]{1,0:T(8,128)}, u32[]{:S(2)}) copy-start(f32[128,1024]{1,0:T(8,128)} %fusion.238) | copy-start | bytes 1572868 | tf_op jit(solution)/shard_map/while
  353.7 8.7 %copy-start.5 = (f32[128,1024]{1,0:T(8,128)S(1)}, f32[128,1024]{1,0:T(8,128)}, u32[]{:S(2)}) copy-start(f32[128,1024]{1,0:T(8,128)} %fusion.229) | copy-start | bytes 1572868 | tf_op jit(solution)/shard_map/while
  353.7 8.7 %copy-start.6 = (f32[128,1024]{1,0:T(8,128)S(1)}, f32[128,1024]{1,0:T(8,128)}, u32[]{:S(2)}) copy-start(f32[128,1024]{1,0:T(8,128)} %fusion.232) | copy-start | bytes 1572868 | tf_op jit(solution)/shard_map/while
  353.7 8.7 %copy-start.7 = (f32[128,1024]{1,0:T(8,128)S(1)}, f32[128,1024]{1,0:T(8,128)}, u32[]{:S(2)}) copy-start(f32[128,1024]{1,0:T(8,128)} %fusion.236) | copy-start | bytes 1572868 | tf_op jit(solution)/shard_map/while
  353.8 8.7 %copy-start.8 = (f32[128,1024]{1,0:T(8,128)S(1)}, f32[128,1024]{1,0:T(8,128)}, u32[]{:S(2)}) copy-start(f32[128,1024]{1,0:T(8,128)} %fusion.228) | copy-start | bytes 1572868 | tf_op jit(solution)/shard_map/while
  353.8 8.7 %copy-start.9 = (f32[128,1024]{1,0:T(8,128)S(1)}, f32[128,1024]{1,0:T(8,128)}, u32[]{:S(2)}) copy-start(f32[128,1024]{1,0:T(8,128)} %fusion.231) | copy-start | bytes 1572868 | tf_op jit(solution)/shard_map/while
  353.8 8.7 %copy-start.10 = (f32[128,1024]{1,0:T(8,128)S(1)}, f32[128,1024]{1,0:T(8,128)}, u32[]{:S(2)}) copy-start(f32[128,1024]{1,0:T(8,128)} %fusion.235) | copy-start | bytes 1572868 | tf_op jit(solution)/shard_map/while
  353.8 8.7 %copy-start.11 = (f32[128,1024]{1,0:T(8,128)S(1)}, f32[128,1024]{1,0:T(8,128)}, u32[]{:S(2)}) copy-start(f32[128,1024]{1,0:T(8,128)} %fusion.234) | copy-start | bytes 1572868 | tf_op jit(solution)/shard_map/while
  353.8 8.7 %copy-start.12 = (f32[128,1024]{1,0:T(8,128)S(1)}, f32[128,1024]{1,0:T(8,128)}, u32[]{:S(2)}) copy-start(f32[128,1024]{1,0:T(8,128)} %get-tuple-element.601) | copy-start | bytes 1572868 | tf_op jit(solution)/shard_map/while
  353.8 8.7 %copy-start.13 = (f32[128,1024]{1,0:T(8,128)S(1)}, f32[128,1024]{1,0:T(8,128)}, u32[]{:S(2)}) copy-start(f32[128,1024]{1,0:T(8,128)} %get-tuple-element.592) | copy-start | bytes 1572868 | tf_op jit(solution)/shard_map/while
  353.8 8.7 %copy-start.14 = (f32[128,1024]{1,0:T(8,128)S(1)}, f32[128,1024]{1,0:T(8,128)}, u32[]{:S(2)}) copy-start(f32[128,1024]{1,0:T(8,128)} %get-tuple-element.596) | copy-start | bytes 1572868 | tf_op jit(solution)/shard_map/while
  390.3 7.9 copy-start.23
  499.4 9.3 %copy-start.15 = (bf16[1,148,8,128]{3,2,0,1:T(8,128)(2,1)S(1)}, bf16[1,148,8,128]{3,2,0,1:T(8,128)(2,1)}, u32[]{:S(2)}) copy-start(bf16[1,148,8,128]{3,2,0,1:T(8,128)(2,1)} %get-tuple-element.604) | copy-start | bytes 909316 | tf_op jit(solution)/shard_map/while
  513.1 8.7 %copy-start.2 = (f32[128,1024]{1,0:T(8,128)S(1)}, f32[128,1024]{1,0:T(8,128)}, u32[]{:S(2)}) copy-start(f32[128,1024]{1,0:T(8,128)} %fusion.230) | copy-start | bytes 1572868 | tf_op jit(solution)/shard_map/while
  513.2 8.7 %copy-start.3 = (f32[128,1024]{1,0:T(8,128)S(1)}, f32[128,1024]{1,0:T(8,128)}, u32[]{:S(2)}) copy-start(f32[128,1024]{1,0:T(8,128)} %fusion.233) | copy-start | bytes 1572868 | tf_op jit(solution)/shard_map/while
  513.2 8.7 %copy-start.4 = (f32[128,1024]{1,0:T(8,128)S(1)}, f32[128,1024]{1,0:T(8,128)}, u32[]{:S(2)}) copy-start(f32[128,1024]{1,0:T(8,128)} %fusion.238) | copy-start | bytes 1572868 | tf_op jit(solution)/shard_map/while
  513.2 8.7 %copy-start.5 = (f32[128,1024]{1,0:T(8,128)S(1)}, f32[128,1024]{1,0:T(8,128)}, u32[]{:S(2)}) copy-start(f32[128,1024]{1,0:T(8,128)} %fusion.229) | copy-start | bytes 1572868 | tf_op jit(solution)/shard_map/while
  513.2 8.7 %copy-start.6 = (f32[128,1024]{1,0:T(8,128)S(1)}, f32[128,1024]{1,0:T(8,128)}, u32[]{:S(2)}) copy-start(f32[128,1024]{1,0:T(8,128)} %fusion.232) | copy-start | bytes 1572868 | tf_op jit(solution)/shard_map/while
  513.2 8.7 %copy-start.7 = (f32[128,1024]{1,0:T(8,128)S(1)}, f32[128,1024]{1,0:T(8,128)}, u32[]{:S(2)}) copy-start(f32[128,1024]{1,0:T(8,128)} %fusion.236) | copy-start | bytes 1572868 | tf_op jit(solution)/shard_map/while
  513.2 8.7 %copy-start.8 = (f32[128,1024]{1,0:T(8,128)S(1)}, f32[128,1024]{1,0:T(8,128)}, u32[]{:S(2)}) copy-start(f32[128,1024]{1,0:T(8,128)} %fusion.228) | copy-start | bytes 1572868 | tf_op jit(solution)/shard_map/while
  513.2 8.7 %copy-start.9 = (f32[128,1024]{1,0:T(8,128)S(1)}, f32[128,1024]{1,0:T(8,128)}, u32[]{:S(2)}) copy-start(f32[128,1024]{1,0:T(8,128)} %fusion.231) | copy-start | bytes 1572868 | tf_op jit(solution)/shard_map/while
  513.2 8.7 %copy-start.10 = (f32[128,1024]{1,0:T(8,128)S(1)}, f32[128,1024]{1,0:T(8,128)}, u32[]{:S(2)}) copy-start(f32[128,1024]{1,0:T(8,128)} %fusion.235) | copy-start | bytes 1572868 | tf_op jit(solution)/shard_map/while
  513.2 8.7 %copy-start.11 = (f32[128,1024]{1,0:T(8,128)S(1)}, f32[128,1024]{1,0:T(8,128)}, u32[]{:S(2)}) copy-start(f32[128,1024]{1,0:T(8,128)} %fusion.234) | copy-start | bytes 1572868 | tf_op jit(solution)/shard_map/while
  513.2 8.7 %copy-start.12 = (f32[128,1024]{1,0:T(8,128)S(1)}, f32[128,1024]{1,0:T(8,128)}, u32[]{:S(2)}) copy-start(f32[128,1024]{1,0:T(8,128)} %get-tuple-element.601) | copy-start | bytes 1572868 | tf_op jit(solution)/shard_map/while
  513.3 8.7 %copy-start.13 = (f32[128,1024]{1,0:T(8,128)S(1)}, f32[128,1024]{1,0:T(8,128)}, u32[]{:S(2)}) copy-start(f32[128,1024]{1,0:T(8,128)} %get-tuple-element.592) | copy-start | bytes 1572868 | tf_op jit(solution)/shard_map/while
  513.3 8.7 %copy-start.14 = (f32[128,1024]{1,0:T(8,128)S(1)}, f32[128,1024]{1,0:T(8,128)}, u32[]{:S(2)}) copy-start(f32[128,1024]{1,0:T(8,128)} %get-tuple-element.596) | copy-start | bytes 1572868 | tf_op jit(solution)/shard_map/while
  549.9 7.9 copy-start.23
  658.9 9.3 %copy-start.15 = (bf16[1,148,8,128]{3,2,0,1:T(8,128)(2,1)S(1)}, bf16[1,148,8,128]{3,2,0,1:T(8,128)(2,1)}, u32[]{:S(2)}) copy-start(bf16[1,148,8,128]{3,2,0,1:T(8,128)(2,1)} %get-tuple-element.604) | copy-start | bytes 909316 | tf_op jit(solution)/shard_map/while
  672.7 8.7 %copy-start.2 = (f32[128,1024]{1,0:T(8,128)S(1)}, f32[128,1024]{1,0:T(8,128)}, u32[]{:S(2)}) copy-start(f32[128,1024]{1,0:T(8,128)} %fusion.230) | copy-start | bytes 1572868 | tf_op jit(solution)/shard_map/while
  672.7 8.7 %copy-start.3 = (f32[128,1024]{1,0:T(8,128)S(1)}, f32[128,1024]{1,0:T(8,128)}, u32[]{:S(2)}) copy-start(f32[128,1024]{1,0:T(8,128)} %fusion.233) | copy-start | bytes 1572868 | tf_op jit(solution)/shard_map/while
  672.7 8.7 %copy-start.4 = (f32[128,1024]{1,0:T(8,128)S(1)}, f32[128,1024]{1,0:T(8,128)}, u32[]{:S(2)}) copy-start(f32[128,1024]{1,0:T(8,128)} %fusion.238) | copy-start | bytes 1572868 | tf_op jit(solution)/shard_map/while
  672.7 8.7 %copy-start.5 = (f32[128,1024]{1,0:T(8,128)S(1)}, f32[128,1024]{1,0:T(8,128)}, u32[]{:S(2)}) copy-start(f32[128,1024]{1,0:T(8,128)} %fusion.229) | copy-start | bytes 1572868 | tf_op jit(solution)/shard_map/while
  672.7 8.7 %copy-start.6 = (f32[128,1024]{1,0:T(8,128)S(1)}, f32[128,1024]{1,0:T(8,128)}, u32[]{:S(2)}) copy-start(f32[128,1024]{1,0:T(8,128)} %fusion.232) | copy-start | bytes 1572868 | tf_op jit(solution)/shard_map/while
  672.7 8.7 %copy-start.7 = (f32[128,1024]{1,0:T(8,128)S(1)}, f32[128,1024]{1,0:T(8,128)}, u32[]{:S(2)}) copy-start(f32[128,1024]{1,0:T(8,128)} %fusion.236) | copy-start | bytes 1572868 | tf_op jit(solution)/shard_map/while
  672.7 8.7 %copy-start.8 = (f32[128,1024]{1,0:T(8,128)S(1)}, f32[128,1024]{1,0:T(8,128)}, u32[]{:S(2)}) copy-start(f32[128,1024]{1,0:T(8,128)} %fusion.228) | copy-start | bytes 1572868 | tf_op jit(solution)/shard_map/while
  672.7 8.7 %copy-start.9 = (f32[128,1024]{1,0:T(8,128)S(1)}, f32[128,1024]{1,0:T(8,128)}, u32[]{:S(2)}) copy-start(f32[128,1024]{1,0:T(8,128)} %fusion.231) | copy-start | bytes 1572868 | tf_op jit(solution)/shard_map/while
  672.7 8.7 %copy-start.10 = (f32[128,1024]{1,0:T(8,128)S(1)}, f32[128,1024]{1,0:T(8,128)}, u32[]{:S(2)}) copy-start(f32[128,1024]{1,0:T(8,128)} %fusion.235) | copy-start | bytes 1572868 | tf_op jit(solution)/shard_map/while
  672.8 8.7 %copy-start.11 = (f32[128,1024]{1,0:T(8,128)S(1)}, f32[128,1024]{1,0:T(8,128)}, u32[]{:S(2)}) copy-start(f32[128,1024]{1,0:T(8,128)} %fusion.234) | copy-start | bytes 1572868 | tf_op jit(solution)/shard_map/while
  672.8 8.7 %copy-start.12 = (f32[128,1024]{1,0:T(8,128)S(1)}, f32[128,1024]{1,0:T(8,128)}, u32[]{:S(2)}) copy-start(f32[128,1024]{1,0:T(8,128)} %get-tuple-element.601) | copy-start | bytes 1572868 | tf_op jit(solution)/shard_map/while
  672.8 8.7 %copy-start.13 = (f32[128,1024]{1,0:T(8,128)S(1)}, f32[128,1024]{1,0:T(8,128)}, u32[]{:S(2)}) copy-start(f32[128,1024]{1,0:T(8,128)} %get-tuple-element.592) | copy-start | bytes 1572868 | tf_op jit(solution)/shard_map/while
  672.8 8.7 %copy-start.14 = (f32[128,1024]{1,0:T(8,128)S(1)}, f32[128,1024]{1,0:T(8,128)}, u32[]{:S(2)}) copy-start(f32[128,1024]{1,0:T(8,128)} %get-tuple-element.596) | copy-start | bytes 1572868 | tf_op jit(solution)/shard_map/while
  709.1 7.9 copy-start.23
  818.3 9.3 %copy-start.15 = (bf16[1,148,8,128]{3,2,0,1:T(8,128)(2,1)S(1)}, bf16[1,148,8,128]{3,2,0,1:T(8,128)(2,1)}, u32[]{:S(2)}) copy-start(bf16[1,148,8,128]{3,2,0,1:T(8,128)(2,1)} %get-tuple-element.604) | copy-start | bytes 909316 | tf_op jit(solution)/shard_map/while
  832.1 8.7 %copy-start.2 = (f32[128,1024]{1,0:T(8,128)S(1)}, f32[128,1024]{1,0:T(8,128)}, u32[]{:S(2)}) copy-start(f32[128,1024]{1,0:T(8,128)} %fusion.230) | copy-start | bytes 1572868 | tf_op jit(solution)/shard_map/while
  832.1 8.7 %copy-start.3 = (f32[128,1024]{1,0:T(8,128)S(1)}, f32[128,1024]{1,0:T(8,128)}, u32[]{:S(2)}) copy-start(f32[128,1024]{1,0:T(8,128)} %fusion.233) | copy-start | bytes 1572868 | tf_op jit(solution)/shard_map/while
  832.1 8.7 %copy-start.4 = (f32[128,1024]{1,0:T(8,128)S(1)}, f32[128,1024]{1,0:T(8,128)}, u32[]{:S(2)}) copy-start(f32[128,1024]{1,0:T(8,128)} %fusion.238) | copy-start | bytes 1572868 | tf_op jit(solution)/shard_map/while
  832.1 8.7 %copy-start.5 = (f32[128,1024]{1,0:T(8,128)S(1)}, f32[128,1024]{1,0:T(8,128)}, u32[]{:S(2)}) copy-start(f32[128,1024]{1,0:T(8,128)} %fusion.229) | copy-start | bytes 1572868 | tf_op jit(solution)/shard_map/while
  832.1 8.7 %copy-start.6 = (f32[128,1024]{1,0:T(8,128)S(1)}, f32[128,1024]{1,0:T(8,128)}, u32[]{:S(2)}) copy-start(f32[128,1024]{1,0:T(8,128)} %fusion.232) | copy-start | bytes 1572868 | tf_op jit(solution)/shard_map/while
  832.1 8.7 %copy-start.7 = (f32[128,1024]{1,0:T(8,128)S(1)}, f32[128,1024]{1,0:T(8,128)}, u32[]{:S(2)}) copy-start(f32[128,1024]{1,0:T(8,128)} %fusion.236) | copy-start | bytes 1572868 | tf_op jit(solution)/shard_map/while
  832.1 8.7 %copy-start.8 = (f32[128,1024]{1,0:T(8,128)S(1)}, f32[128,1024]{1,0:T(8,128)}, u32[]{:S(2)}) copy-start(f32[128,1024]{1,0:T(8,128)} %fusion.228) | copy-start | bytes 1572868 | tf_op jit(solution)/shard_map/while
  832.1 8.7 %copy-start.9 = (f32[128,1024]{1,0:T(8,128)S(1)}, f32[128,1024]{1,0:T(8,128)}, u32[]{:S(2)}) copy-start(f32[128,1024]{1,0:T(8,128)} %fusion.231) | copy-start | bytes 1572868 | tf_op jit(solution)/shard_map/while
  832.2 8.7 %copy-start.10 = (f32[128,1024]{1,0:T(8,128)S(1)}, f32[128,1024]{1,0:T(8,128)}, u32[]{:S(2)}) copy-start(f32[128,1024]{1,0:T(8,128)} %fusion.235) | copy-start | bytes 1572868 | tf_op jit(solution)/shard_map/while
  832.2 8.7 %copy-start.11 = (f32[128,1024]{1,0:T(8,128)S(1)}, f32[128,1024]{1,0:T(8,128)}, u32[]{:S(2)}) copy-start(f32[128,1024]{1,0:T(8,128)} %fusion.234) | copy-start | bytes 1572868 | tf_op jit(solution)/shard_map/while
  832.2 8.7 %copy-start.12 = (f32[128,1024]{1,0:T(8,128)S(1)}, f32[128,1024]{1,0:T(8,128)}, u32[]{:S(2)}) copy-start(f32[128,1024]{1,0:T(8,128)} %get-tuple-element.601) | copy-start | bytes 1572868 | tf_op jit(solution)/shard_map/while
  832.2 8.7 %copy-start.13 = (f32[128,1024]{1,0:T(8,128)S(1)}, f32[128,1024]{1,0:T(8,128)}, u32[]{:S(2)}) copy-start(f32[128,1024]{1,0:T(8,128)} %get-tuple-element.592) | copy-start | bytes 1572868 | tf_op jit(solution)/shard_map/while
  832.2 8.7 %copy-start.14 = (f32[128,1024]{1,0:T(8,128)S(1)}, f32[128,1024]{1,0:T(8,128)}, u32[]{:S(2)}) copy-start(f32[128,1024]{1,0:T(8,128)} %get-tuple-element.596) | copy-start | bytes 1572868 | tf_op jit(solution)/shard_map/while
  (65 other events, 278.1 us)
Sparse Core Ops, SparseCore 0:
  9.2 39.4 all-gather.1
where the time goes:
time: 869 us; the launch traced here: 856 us
  matrix products  419 us (48%)
  local copies, waits for them, and re-layouts  325 us (37%)
  other arithmetic  63.9 us (7%)
  waiting for transfers between devices  23.2 us (3%)
  between operations  14.3 us (2%)
    dot_general x44, matrix products, one_group(): jnp.einsum('km,kyx->myx', weights, convolved, precision=lax.Precision.HIG...  340 us
    gather x96, local copies, waits for them, and re-layouts  135 us
    dot_general x56, local copies, waits for them, and re-layouts, one_group(): jnp.einsum('kyr,rx->kyx', kernels, across_all[first_factor + across_pow],...  104 us
    dot_general x56, matrix products, one_group(): jnp.einsum('kyr,rx->kyx', kernels, across_all[first_factor + across_pow],...  55 us
    another operation x12, local copies, waits for them, and re-layouts, one_group(): jnp.stack([jnp.ones_like(xgrid), xgrid, ygrid, xgrid * xgrid, xgrid * ygr...  44.9 us
    reduce_sum x4, other arithmetic, one_group(): psf_part = psf_part + jnp.sum(folded * poly_terms, axis=0)  31.7 us
    all_gather x1, waiting for transfers between devices, per_device(): lax.all_gather(patches.astype(jnp.bfloat16), 'ccd', axis=0, tiled=True)  19.8 us
  transfers between devices with their start and end apart: 3, of which 2 were waited for; matrix products, arithmetic and copies ran while one was open for 3% of the time, Pallas kernels for 0%

commit v1 on v0

v1 whole, which is shorter than its diff:
```python
import functools

import jax
import jax.numpy as jnp
import ml_dtypes
import numpy as np
from jax import lax
from jax.experimental import pallas as pl
from jax.experimental.pallas import tpu as pltpu
from jax.sharding import PartitionSpec as P

TS = 128
HALF = 10
RIM = 16
WINDOW = 2 * TS
VMEM_BYTES = 48 * 2**20

gauss_widths = (1.0, 2.0, 4.0)
poly_degrees = (4, 4, 3)
poly_powers = ((0, 0), (1, 0), (0, 1), (2, 0), (1, 1), (0, 2))
QMAX = max(poly_degrees) + 1


def factor_table():
    offsets = np.arange(-HALF, HALF + 1).astype(np.float64)
    shapes = []
    for sigma_px, degree in zip(gauss_widths, poly_degrees):
        for exponent in range(degree + 1):
            profile = np.exp(-offsets * offsets / (2.0 * sigma_px * sigma_px))
            profile = profile * (offsets / HALF) ** exponent
            shapes.append(profile / np.sum(np.abs(profile)))
    return np.stack(shapes).astype(np.float32).astype(ml_dtypes.bfloat16).astype(np.float32)


def across_pairs():
    return [(s, p) for s, degree in enumerate(poly_degrees) for p in range(degree + 1)]


def banded(taps, lags):
    inside = np.abs(lags) <= HALF
    return np.where(inside, taps[np.clip(lags + HALF, 0, 2 * HALF)], 0.0)


def across_matrix():
    factors = factor_table()
    lags = np.arange(WINDOW)[:, None] - TS // 2 - np.arange(TS)[None, :]
    return np.concatenate([banded(f, lags) for f in factors], axis=1).astype(ml_dtypes.bfloat16)


def down_factors(lags):
    factors = factor_table()
    first = np.concatenate([[0], np.cumsum([d + 1 for d in poly_degrees])])
    out = []
    for q in range(QMAX):
        row = []
        for s, p in across_pairs():
            if q <= poly_degrees[s]:
                row.append(banded(factors[first[s] + q], lags))
            else:
                row.append(np.zeros(lags.shape))
        out.append(np.concatenate(row, axis=1))
    return np.stack(out).astype(ml_dtypes.bfloat16)


def basis_select():
    pairs = across_pairs()
    select = np.zeros((QMAX, len(pairs), sum(d + 1 - p for d in poly_degrees for p in range(d + 1))))
    k = 0
    for h, (s, p) in enumerate(pairs):
        for q in range(poly_degrees[s] + 1 - p):
            select[q, h, k] = 1.0
            k += 1
    return select.astype(np.float32)


def weights_kernel(c_ref, y_ref, d_ref, out_ref):
    yh = y_ref[...]
    factors = [d_ref[q].astype(jnp.float32) for q in range(QMAX)]
    for a in range(3):
        total = None
        for m, (xp, yp) in enumerate(poly_powers):
            if xp != a:
                continue
            term = None
            for q in range(QMAX):
                part = c_ref[m * QMAX + q : m * QMAX + q + 1, :] * factors[q]
                term = part if term is None else term + part
            for _ in range(yp):
                term = term * yh
            total = term if total is None else total + term
        out_ref[a] = total.astype(out_ref.dtype)


def build_weights(coeff_lanes, ycol, down, lanes):
    rows, width = down.shape[1:]
    return pl.pallas_call(
        weights_kernel,
        grid=(width // lanes,),
        in_specs=[
            pl.BlockSpec((coeff_lanes.shape[0], lanes), lambda i: (0, i)),
            pl.BlockSpec((rows, 1), lambda i: (0, 0)),
            pl.BlockSpec((QMAX, rows, lanes), lambda i: (0, 0, i)),
        ],
        out_specs=pl.BlockSpec((3, rows, lanes), lambda i: (0, 0, i)),
        out_shape=jax.ShapeDtypeStruct((3, rows, width), jnp.bfloat16),
        compiler_params=pltpu.CompilerParams(vmem_limit_bytes=VMEM_BYTES),
        cost_estimate=pl.CostEstimate(
            flops=40 * 2 * rows * width, bytes_accessed=16 * rows * width, transcendentals=0
        ),
    )(coeff_lanes, ycol, down)


def crop_kernel(per_step, owner, patch, row_shift, col_shift, *refs):
    patch_refs, out_ref, carry = refs[:per_step], refs[per_step], refs[per_step + 1]
    step = pl.program_id(0)

    @pl.when(step == 0)
    def _():
        carry[...] = jnp.zeros_like(carry)

    row_lag = lax.broadcasted_iota(jnp.int32, (TS, 2 * TS), 1) - lax.broadcasted_iota(
        jnp.int32, (TS, 2 * TS), 0
    )
    col_lag = lax.broadcasted_iota(jnp.int32, (2 * TS, 2 * TS), 0) - lax.broadcasted_iota(
        jnp.int32, (2 * TS, 2 * TS), 1
    )
    column = lax.broadcasted_iota(jnp.int32, (2 * TS, 2 * TS), 1)
    held = (column >= TS // 2) & (column < TS // 2 + TS)
    col_lag = jnp.where(held, col_lag + TS // 2, -1)
    before = carry[...]
    for j in range(per_step):
        t = step * per_step + j
        pick_rows = (row_lag == row_shift[t]).astype(jnp.float32).astype(jnp.bfloat16)
        pick_cols = (col_lag == col_shift[t]).astype(jnp.float32).astype(jnp.bfloat16)
        rows = jnp.dot(pick_rows, patch_refs[j][0, 0, 0], preferred_element_type=jnp.float32)
        wide = jnp.dot(
            rows.astype(jnp.bfloat16), pick_cols, preferred_element_type=jnp.float32
        ).astype(jnp.bfloat16)
        first = pl.multiple_of(t * TS, TS)
        out_ref[:, pl.ds(first, TS)] = before + wide[:, :TS]
        before = wide[:, TS:]
    carry[...] = before

    @pl.when(step == pl.num_programs(0) - 1)
    def _():
        out_ref[:, out_ref.shape[1] - TS :] = before


def crop(piece, owner, patch, row_shift, col_shift):
    tiles = owner.shape[0]
    per_step = 8

    def block(j):
        return pl.BlockSpec(
            (1, 1, 1, 2 * TS, 2 * TS),
            lambda i, own, pat, dy, dx: (own[i * per_step + j], 0, pat[i * per_step + j], 0, 0),
        )

    width = (tiles + 1) * TS
    return pl.pallas_call(
        functools.partial(crop_kernel, per_step),
        grid_spec=pltpu.PrefetchScalarGridSpec(
            num_scalar_prefetch=4,
            grid=(tiles // per_step,),
            in_specs=[block(j) for j in range(per_step)],
            out_specs=pl.BlockSpec((TS, width), lambda i, *_: (0, 0)),
            scratch_shapes=[pltpu.VMEM((TS, TS), jnp.bfloat16)],
        ),
        out_shape=jax.ShapeDtypeStruct((TS, width), jnp.bfloat16),
        compiler_params=pltpu.CompilerParams(vmem_limit_bytes=VMEM_BYTES),
        cost_estimate=pl.CostEstimate(
            flops=tiles * 2 * TS * 8 * TS * TS, bytes_accessed=5 * 2**20, transcendentals=0
        ),
    )(owner, patch, row_shift, col_shift, *([piece] * per_step))


def apply_factors(windows, across_ref, weights, spread, columns, first_column):
    rows = windows[0].shape[0]
    stacked = jnp.concatenate(windows, axis=0)
    for pair in range(across_ref.shape[1] // WINDOW):
        result = jnp.dot(
            stacked,
            across_ref[:, pair * WINDOW : (pair + 1) * WINDOW],
            preferred_element_type=jnp.float32,
        ).astype(jnp.bfloat16)
        for b in range(len(windows)):
            for half in range(2):
                h = 2 * pair + half
                spread[h * rows : (h + 1) * rows, b * TS : (b + 1) * TS] = result[
                    b * rows : (b + 1) * rows, half * TS : (half + 1) * TS
                ]
    folded = jnp.dot(weights, spread[...], preferred_element_type=jnp.float32)
    out_rows = weights.shape[0] // 3
    width = len(windows) * TS
    position = first_column + lax.broadcasted_iota(jnp.int32, (1, width), 1)
    xh = (2.0 * position.astype(jnp.float32) + 1.0) / columns - 1.0
    return folded[:out_rows] + xh * (
        folded[out_rows : 2 * out_rows] + xh * folded[2 * out_rows :]
    )


def centre_kernel(columns, template_ref, across_ref, weight_ref, science_ref, out_ref, spread):
    width = out_ref.shape[1]
    first = pl.program_id(0) * width
    windows = [
        template_ref[:, pl.ds(pl.multiple_of(first + b * TS, TS), WINDOW)]
        for b in range(width // TS)
    ]
    weights = weight_ref[...].reshape(-1, weight_ref.shape[2])
    psf = apply_factors(windows, across_ref, weights, spread, columns, first)
    out_ref[...] = science_ref[...] - psf


def centre(template, across, weights, science, width):
    rows, columns = science.shape
    return pl.pallas_call(
        functools.partial(centre_kernel, columns),
        grid=(columns // width,),
        in_specs=[
            pl.BlockSpec(template.shape, lambda i: (0, 0)),
            pl.BlockSpec(across.shape, lambda i: (0, 0)),
            pl.BlockSpec(weights.shape, lambda i: (0, 0, 0)),
            pl.BlockSpec((rows, width), lambda i: (0, i)),
        ],
        out_specs=pl.BlockSpec((rows, width), lambda i: (0, i)),
        out_shape=jax.ShapeDtypeStruct(science.shape, jnp.float32),
        scratch_shapes=[pltpu.VMEM((weights.shape[2], width), jnp.bfloat16)],
        compiler_params=pltpu.CompilerParams(vmem_limit_bytes=VMEM_BYTES),
        cost_estimate=pl.CostEstimate(
            flops=2 * columns * weights.shape[2] * (3 * rows + WINDOW),
            bytes_accessed=8 * rows * columns + 4 * 2**20,
            transcendentals=0,
        ),
    )(template, across, weights, science)


def rim_kernel(columns, top_ref, low_ref, across_ref, weight_ref, held_ref, out_ref, spread):
    width = out_ref.shape[1]
    first = pl.program_id(1) * width
    is_top = pl.program_id(0) == 0
    windows = []
    for b in range(width // TS):
        where = pl.ds(pl.multiple_of(first + b * TS, TS), WINDOW)
        windows.append(jnp.where(is_top, top_ref[:, where], low_ref[:, where]))
    weights = weight_ref[...].reshape(-1, weight_ref.shape[2])
    psf = apply_factors(windows, across_ref, weights, spread, columns, first)
    out_ref[...] = held_ref[...] - psf


def rims(top, low, across, weights, held, width):
    rows, columns = held.shape
    last = rows // RIM - 1
    return pl.pallas_call(
        functools.partial(rim_kernel, columns),
        grid=(2, columns // width),
        in_specs=[
            pl.BlockSpec(top.shape, lambda v, i: (0, 0)),
            pl.BlockSpec(low.shape, lambda v, i: (0, 0)),
            pl.BlockSpec(across.shape, lambda v, i: (0, 0)),
            pl.BlockSpec((3, RIM, weights.shape[2]), lambda v, i: (0, v, 0)),
            pl.BlockSpec((RIM, width), lambda v, i: (v * last, i)),
        ],
        out_specs=pl.BlockSpec((RIM, width), lambda v, i: (v * last, i)),
        out_shape=jax.ShapeDtypeStruct(held.shape, jnp.float32),
        scratch_shapes=[pltpu.VMEM((weights.shape[2], width), jnp.bfloat16)],
        input_output_aliases={4: 0},
        compiler_params=pltpu.CompilerParams(vmem_limit_bytes=VMEM_BYTES),
        cost_estimate=pl.CostEstimate(
            flops=4 * columns * weights.shape[2] * (3 * RIM + WINDOW),
            bytes_accessed=2**20,
            transcendentals=0,
        ),
    )(top, low, across, weights, held)


def per_device(science, patches, coeffs, tile_owner, tile_patch, tile_offset):
    ccd_id = lax.axis_index("ccd")
    amp_id = lax.axis_index("amp")
    amp_count = lax.axis_size("amp")
    strip_rows, columns = science.shape[1:]

    piece = lax.all_gather(patches.astype(jnp.bfloat16), "ccd", axis=0, tiled=True)

    owner = tile_owner[ccd_id, amp_id, :, 0]
    patch = tile_patch[ccd_id, amp_id]
    row_shift = tile_offset[ccd_id, amp_id, :, 0]
    col_shift = tile_offset[ccd_id, amp_id, :, 1]

    across = jnp.asarray(across_matrix())
    row = np.arange(strip_rows)
    centre_down = down_factors(row[None, :] - row[:, None])
    rim_row = np.arange(RIM)
    top_lags = (rim_row[None, :] - RIM) - rim_row[:, None]
    low_lags = (rim_row[None, :] + RIM) - rim_row[:, None]
    rim_down = np.concatenate([down_factors(top_lags), down_factors(low_lags)], axis=1)
    select = jnp.asarray(basis_select())
    coeff_table = jnp.einsum("qhk,km->mqh", select, coeffs[0], precision=lax.Precision.HIGHEST)
    coeff_table = coeff_table.reshape(-1, coeff_table.shape[2])
    ycoord = (
        2.0 * (amp_id * strip_rows + jnp.arange(strip_rows)).astype(jnp.float32) + 1.0
    ) / (amp_count * strip_rows) - 1.0
    ycol = ycoord[:, None]
    centre_weights = build_weights(
        jnp.repeat(coeff_table, strip_rows, axis=1), ycol, jnp.asarray(centre_down), 2 * strip_rows
    )
    rim_weights = build_weights(
        jnp.repeat(coeff_table, RIM, axis=1),
        jnp.concatenate([ycol[:RIM], ycol[-RIM:]], axis=0),
        jnp.asarray(rim_down),
        rim_down.shape[2],
    )

    template = crop(piece, owner, patch, row_shift, col_shift)
    forward = [(i, i + 1) for i in range(amp_count - 1)]
    backward = [(i + 1, i) for i in range(amp_count - 1)]
    top = lax.ppermute(template[-RIM:], "amp", forward)
    low = lax.ppermute(template[:RIM], "amp", backward)
    inner = centre(template, across, centre_weights, science[0], 8 * TS)
    return rims(top, low, across, rim_weights, inner, 16 * TS)[None]


def solution(mesh):
    placed = (
        P("ccd", "amp", None),
        P("ccd", "amp", None, None, None),
        P("ccd", None, None),
        P(),
        P(),
        P(),
    )
    return jax.shard_map(
        per_device, mesh=mesh, in_specs=placed, out_specs=P("ccd", "amp", None), check_vma=False
    )
```

time: 869 us -> 82.8 us (0.10); the launches traced: 856 us -> 82.5 us
  matrix products: 419 us -> 1.03 us
  local copies, waits for them, and re-layouts: 325 us -> 4.65 us
  other arithmetic: 63.9 us -> 2.34 us
  Pallas kernels: 0 us -> 23 us
  waiting for transfers between devices: 23.2 us -> 33.2 us
    dot_general x114 -> x1, matrix products: 419 us -> 1.03 us  [per_device(): jnp.einsum('qhk,km->mqh', select, coeffs[0], precision=lax.Precision.HIGH...]
    gather x96 -> x0, local copies, waits for them, and re-layouts: 135 us -> none
    dot_general x56 -> x1, local copies, waits for them, and re-layouts: 104 us -> 0.02 us  [per_device(): jnp.einsum('qhk,km->mqh', select, coeffs[0], precision=lax.Precision.HIGH...]
    another operation x18 -> x0, local copies, waits for them, and re-layouts: 49.3 us -> none  [the longest x12 44.9 us: one_group(): jnp.stack([jnp.ones_like(xgrid), xgrid, ygrid, xgrid * xgrid, xgrid * ygr...]
    reduce_sum x18 -> x0, other arithmetic: 40.7 us -> none  [the longest x4 31.7 us: one_group(): psf_part = psf_part + jnp.sum(folded * poly_terms, axis=0)]
    pallas_call x0 -> x5, Pallas kernels: none -> 23 us  [the longest x1 12.3 us: centre(): pl.pallas_call(functools.partial(centre_kernel, columns), grid=(columns /...]
    all_gather x1, waiting for transfers between devices: 19.8 us -> 33.2 us  [per_device(): lax.all_gather(patches.astype(jnp.bfloat16), 'ccd', axis=0, tiled=True)]
    slice x12 -> x2, local copies, waits for them, and re-layouts: 10.5 us -> 0.09 us  [the longest x1 0.07 us: per_device(): ycol[:RIM]]
  transfers between devices with their start and end apart: 3 -> 3, of which waited for: 2 -> 1; matrix products, arithmetic and copies ran while one was open for 3% -> 3% of each run, Pallas kernels for 0% -> 19%
where the time goes in v1:
time: 82.8 us; the launch traced here: 82.5 us
  waiting for transfers between devices  33.2 us (40%)
  Pallas kernels  23 us (28%)
  between operations  13.6 us (16%)
  starting transfers between devices  4.72 us (6%)
  local copies, waits for them, and re-layouts  4.65 us (6%)
  other arithmetic  2.34 us (3%)
  matrix products  1.03 us (1%)
    all_gather x1, waiting for transfers between devices, per_device(): lax.all_gather(patches.astype(jnp.bfloat16), 'ccd', axis=0, tiled=True)  33.2 us
    pallas_call x1, Pallas kernels, centre(): pl.pallas_call(functools.partial(centre_kernel, columns), grid=(columns /...  12.3 us
    pallas_call x1, Pallas kernels, rims(): pl.pallas_call(functools.partial(rim_kernel, columns), grid=(2, columns /...  4.77 us
    ppermute x1, starting transfers between devices, per_device(): top = lax.ppermute(template[-RIM:], 'amp', forward)  3.4 us
    unnamed x20, local copies, waits for them, and re-layouts  3.38 us
    pallas_call x2, Pallas kernels, build_weights(): pl.pallas_call(weights_kernel, grid=(width // lanes,), in_specs=[pl.Block...  3.07 us
    pallas_call x1, Pallas kernels, crop(): pl.pallas_call(functools.partial(crop_kernel, per_step), grid_spec=pltpu....  2.93 us
    convert_element_type x1, other arithmetic, per_device(): patches.astype(jnp.bfloat16)  2.23 us
  transfers between devices with their start and end apart: 3, of which 1 were waited for; matrix products, arithmetic and copies ran while one was open for 3% of the time, Pallas kernels for 19%

profile of v1, /device:TPU:0, one launch (start us, length us, event | category | flops | bytes accessed | tf_op | source)
XLA Modules:
  0.0 82.5 jit_solution(16126759827830039050)
XLA Ops:
  6.5 0.0 copy-start
  6.5 0.0 copy-start.8
  6.5 0.0 copy-start.6
  6.5 0.0 copy-start.2
  6.5 0.0 all-gather.2.cloned.1.call-start
  6.6 2.2 %convert_element_type.15 = bf16[1,1,4,256,256]{4,3,2,1,0:T(8,128)(2,1)} convert(f32[1,1,4,256,256]{4,3,2,1,0:T(8,128)} %param.11) | non-fusion elementwise | flops 262144 | bytes 1572864 | tf_op jit(solution)/shard_map/convert_element_type | solution.py:282
  8.8 0.0 all-gather.2.cloned.1.call-update
  8.8 0.0 copy-done.8
  8.9 1.0 %convolution_bitcast_fusion = f32[6,5,14]{2,0,1:T(8,128)S(1)} fusion(f32[5,14,40]{2,1,0:T(8,128)S(1)} %copy-done.8, f32[1,40,6]{1,0,2:T(1,128)} %param.12), kind=kOutput, calls=%fused_computation | convolution fusion | flops 201600 | bytes 13840 | tf_op jit(solution)/shard_map/qhk,km->mqh/dot_general | solution.py:297
  9.9 0.1 copy.24
  10.0 0.1 broadcast_in_dim.11
  10.2 0.1 copy.29
  10.3 0.1 slice_bitcast_fusion.1
  10.3 0.1 pad_maximum_fusion
  10.4 0.1 copy.26.y_ref
  10.5 0.1 copy.25.c_ref
  10.6 0.0 copy-done.6
  10.6 0.1 shard_map.101.weight_ref
  10.7 0.0 copy-done.2
  10.7 3.0 %shard_map.102.weight_ref = bf16[3,128,1792]{2,1,0:T(8,128)(2,1)S(1)} custom-call(f32[30,1792]{1,0:T(8,128)S(1)} %bitcast.24, f32[128,1]{1,0:T(8,128)S(1)} %multiply_add_fusion.y_ref, bf16[5,128,1792]{2,1,0:T(8,128)(2,1)S(1)} %copy-done.2), custom_call_target="tpu_custom_call" | custom-call | flops 18350080 | bytes 3670016 | tf_op jit(solution)/shard_map/pallas_call | solution.py:96
  13.7 0.0 copy-start.3
  13.7 1.1 %copy-done.3 = bf16[3,128,1792]{2,1,0:T(8,128)(2,1)} copy-done((bf16[3,128,1792]{2,1,0:T(8,128)(2,1)}, bf16[3,128,1792]{2,1,0:T(8,128)(2,1)S(1)}, u32[]{:S(2)}) %copy-start.3) | copy-done | bytes 1376280
  14.8 0.0 copy-done
  14.8 0.8 fusion.5
  15.6 33.2 %all-gather.2.cloned.1.call-done.refs_0_.refs_1_.refs_2_.refs_3_.refs_4_.refs_5_.refs_6_.refs_7_ = bf16[8,1,4,256,256]{4,3,2,1,0:T(8,128)(2,1)} async-done(((bf16[1,1,4,256,256]{4,3,2,1,0:T(8,128)(2,1)}), bf16[8,1,4,256,256]{4,3,2,1,0:T(8,128)(2,1)}) %all-gather.2.cloned.1.call-update) | async-done | bytes 4194320 | tf_op jit(solution)/shard_map/all_gather | solution.py:282
  48.7 0.0 copy-start.1
  48.7 2.2 %copy-done.1 = bf16[8,1,4,256,256]{4,3,2,1,0:T(8,128)(2,1)S(1)} copy-done((bf16[8,1,4,256,256]{4,3,2,1,0:T(8,128)(2,1)S(1)}, bf16[8,1,4,256,256]{4,3,2,1,0:T(8,128)(2,1)}, u32[]{:S(2)}) %copy-start.1) | copy-done | bytes 4194328
  50.9 0.0 copy-start.4
  50.9 0.0 copy-start.5
  50.9 0.0 copy-start.7
  50.9 2.9 %shard_map.100.template_ref = bf16[128,4224]{1,0:T(8,128)(2,1)S(1)} custom-call(s32[32]{0:T(128)S(1)} %get-tuple-element.11.owner, s32[32]{0:T(128)S(1)} %fusion.3.patch, s32[32]{0:T(128)S(1)} %get-tuple-element.8.row_shift, s32[32]{0:T(128)S(1)} %get-tuple-element.7.col_shift, bf16[8,1,4,256,256]{4,3,2,1,0:T(8,128)(2,1)S(1)} %copy-done.1, ...), custom_call_target="tpu_custom_call" | custom-call | flops 1073741824 | bytes 5242880 | tf_op jit(solution)/shard_map/pallas_call | solution.py:160
  53.9 3.4 %collective-permute-start = (bf16[16,4224]{1,0:T(8,128)(2,1)S(1)}, bf16[16,4224]{1,0:T(8,128)(2,1)S(1)}, u32[]{:S(2)}, u32[]{:S(2)}) collective-permute-start(bf16[16,4224]{1,0:T(8,128)(2,1)S(1)} %get-tuple-element.6), channel_id=1, source_target_pairs={{0,1},{1,2},{2,3},{4,5},{5,6},{6,7},{8,9},{9,10},{10,11},{12,13},{... | collective-permute-start | bytes 405512 | tf_op jit(solution)/shard_map/ppermute | solution.py:316
  57.3 1.3 %collective-permute-start.1 = (bf16[16,4224]{1,0:T(8,128)(2,1)S(1)}, bf16[16,4224]{1,0:T(8,128)(2,1)S(1)}, u32[]{:S(2)}, u32[]{:S(2)}) collective-permute-start(bf16[16,4224]{1,0:T(8,128)(2,1)S(1)} %get-tuple-element.5), channel_id=1, source_target_pairs={{1,0},{2,1},{3,2},{5,4},{6,5},{7,6},{9,8},{10,9},{11,10},{13,12},{... | collective-permute-start | bytes 405512 | tf_op jit(solution)/shard_map/ppermute | solution.py:317
  58.6 0.0 copy-done.4
  58.6 0.0 copy-done.5
  58.6 0.0 copy-done.7
  58.6 12.3 %shard_map.103.held_ref = f32[128,4096]{1,0:T(8,128)} custom-call(bf16[128,4224]{1,0:T(8,128)(2,1)S(1)} %shard_map.100.template_ref, bf16[256,1792]{1,0:T(8,128)(2,1)S(1)} %copy-done.5, bf16[3,128,1792]{2,1,0:T(8,128)(2,1)S(1)} %copy-done.4, f32[128,4096]{1,0:T(8,128)S(1)} %bitcast.25), custom_call_target="tpu_custom_call" | custom-call | flops 9395240960 | bytes 8388608 | tf_op jit(solution)/shard_map/pallas_call | solution.py:216
  70.9 0.0 collective-permute-done.top_ref
  70.9 0.0 collective-permute-done.1.low_ref
  70.9 4.8 %shard_map.104 = f32[128,4096]{1,0:T(8,128)} custom-call(bf16[16,4224]{1,0:T(8,128)(2,1)S(1)} %collective-permute-done.top_ref, bf16[16,4224]{1,0:T(8,128)(2,1)S(1)} %collective-permute-done.1.low_ref, bf16[256,1792]{1,0:T(8,128)(2,1)S(1)} %copy-done.5, bf16[3,32,224]{2,1,0:T(8,128)(2,1)S(1)} %shard_map.101.weight_ref, ...), custom_call_target="tpu_custom_call", output_to_operand_aliasing={{}: (4, {})} | custom-call | flops 1115684864 | bytes 1048576 | tf_op jit(solution)/shard_map/pallas_call | solution.py:253
  (8 shorter events, 0.1 us)
Async XLA Ops:
  6.5 8.3 %copy-start = (s32[8,4,32]{2,1,0:T(4,128)S(1)}, s32[8,4,32]{2,1,0:T(4,128)}, u32[]{:S(2)}) copy-start(s32[8,4,32]{2,1,0:T(4,128)} %param.14) | copy-start | bytes 12292
  6.5 2.3 %copy-start.8 = (f32[5,14,40]{2,1,0:T(8,128)S(1)}, f32[5,14,40]{2,1,0:T(8,128)}, u32[]{:S(2)}) copy-start(f32[5,14,40]{2,1,0:T(8,128)} %constant.37.clone) | copy-start | bytes 33604
  6.5 4.1 %copy-start.6 = (bf16[5,32,224]{2,1,0:T(8,128)(2,1)S(1)}, bf16[5,32,224]{2,1,0:T(8,128)(2,1)}, u32[]{:S(2)}) copy-start(bf16[5,32,224]{2,1,0:T(8,128)(2,1)} %constant.39.clone.d_ref) | copy-start | bytes 215044
  6.5 4.2 %copy-start.2 = (bf16[5,128,1792]{2,1,0:T(8,128)(2,1)S(1)}, bf16[5,128,1792]{2,1,0:T(8,128)(2,1)}, u32[]{:S(2)}) copy-start(bf16[5,128,1792]{2,1,0:T(8,128)(2,1)} %constant.38.clone.d_ref) | copy-start | bytes 6881284
  6.5 42.2 %all-gather.2.cloned.1.call-start = ((), (), s32[]{:S(2)}) async-start(), calls=%async_computation | async-start | bytes 4718592 | tf_op jit(solution)/shard_map/all_gather | solution.py:282
  13.7 1.1 %copy-start.3 = (bf16[3,128,1792]{2,1,0:T(8,128)(2,1)}, bf16[3,128,1792]{2,1,0:T(8,128)(2,1)S(1)}, u32[]{:S(2)}) copy-start(bf16[3,128,1792]{2,1,0:T(8,128)(2,1)S(1)} %shard_map.102.weight_ref) | copy-start | bytes 4128772
  48.7 2.2 %copy-start.1 = (bf16[8,1,4,256,256]{4,3,2,1,0:T(8,128)(2,1)S(1)}, bf16[8,1,4,256,256]{4,3,2,1,0:T(8,128)(2,1)}, u32[]{:S(2)}) copy-start(bf16[8,1,4,256,256]{4,3,2,1,0:T(8,128)(2,1)} %all-gather.2.cloned.1.call-done.refs_0_.refs_1_.refs_2_.refs_3_.refs_4_.refs_5_.refs_6_.refs_7_) | copy-start | bytes 12582916
  50.9 7.7 %copy-start.4 = (bf16[3,128,1792]{2,1,0:T(8,128)(2,1)S(1)}, bf16[3,128,1792]{2,1,0:T(8,128)(2,1)}, u32[]{:S(2)}) copy-start(bf16[3,128,1792]{2,1,0:T(8,128)(2,1)} %copy-done.3) | copy-start | bytes 4128772
  50.9 7.7 %copy-start.5 = (bf16[256,1792]{1,0:T(8,128)(2,1)S(1)}, bf16[256,1792]{1,0:T(8,128)(2,1)}, u32[]{:S(2)}) copy-start(bf16[256,1792]{1,0:T(8,128)(2,1)} %constant.36.clone.across_ref) | copy-start | bytes 2752516
  50.9 7.7 %copy-start.7 = (f32[1,128,4096]{2,1,0:T(8,128)S(1)}, f32[1,128,4096]{2,1,0:T(8,128)}, u32[]{:S(2)}) copy-start(f32[1,128,4096]{2,1,0:T(8,128)} %param.10) | copy-start | bytes 6291460
  53.9 17.0 %collective-permute-start = (bf16[16,4224]{1,0:T(8,128)(2,1)S(1)}, bf16[16,4224]{1,0:T(8,128)(2,1)S(1)}, u32[]{:S(2)}, u32[]{:S(2)}) collective-permute-start(bf16[16,4224]{1,0:T(8,128)(2,1)S(1)} %get-tuple-element.6), channel_id=1, source_target_pairs={{0,1},{1,2},{2,3},{4,5},{5,6},{6,7},{8,9},{9,10},{10,11},{12,13},{... | collective-permute-start | bytes 405512 | tf_op jit(solution)/shard_map/ppermute | solution.py:316
  57.3 13.6 %collective-permute-start.1 = (bf16[16,4224]{1,0:T(8,128)(2,1)S(1)}, bf16[16,4224]{1,0:T(8,128)(2,1)S(1)}, u32[]{:S(2)}, u32[]{:S(2)}) collective-permute-start(bf16[16,4224]{1,0:T(8,128)(2,1)S(1)} %get-tuple-element.5), channel_id=1, source_target_pairs={{1,0},{2,1},{3,2},{5,4},{6,5},{7,6},{9,8},{10,9},{11,10},{13,12},{... | collective-permute-start | bytes 405512 | tf_op jit(solution)/shard_map/ppermute | solution.py:317
Sparse Core Ops, SparseCore 0:
  9.3 39.4 all-gather.1

commit v2 on v1

v2 whole, which is shorter than its diff:
```python
import functools

import jax
import jax.numpy as jnp
import ml_dtypes
import numpy as np
from jax import lax
from jax.experimental import pallas as pl
from jax.experimental.pallas import tpu as pltpu
from jax.sharding import PartitionSpec as P

TS = 128
HALF = 10
RIM = 16
WINDOW = 2 * TS
VMEM_BYTES = 48 * 2**20

gauss_widths = (1.0, 2.0, 4.0)
poly_degrees = (4, 4, 3)
poly_powers = ((0, 0), (1, 0), (0, 1), (2, 0), (1, 1), (0, 2))


def factor_table():
    offsets = np.arange(-HALF, HALF + 1).astype(np.float64)
    shapes = []
    for sigma_px, degree in zip(gauss_widths, poly_degrees):
        for exponent in range(degree + 1):
            profile = np.exp(-offsets * offsets / (2.0 * sigma_px * sigma_px))
            profile = profile * (offsets / HALF) ** exponent
            shapes.append(profile / np.sum(np.abs(profile)))
    return np.stack(shapes).astype(np.float32).astype(ml_dtypes.bfloat16).astype(np.float32)


def across_pairs():
    return [(s, p) for s, degree in enumerate(poly_degrees) for p in range(degree + 1)]


def banded(taps, lags):
    inside = np.abs(lags) <= HALF
    return np.where(inside, taps[np.clip(lags + HALF, 0, 2 * HALF)], 0.0)


def across_matrix():
    factors = factor_table()
    lags = np.arange(WINDOW)[:, None] - TS // 2 - np.arange(TS)[None, :]
    return np.concatenate([banded(f, lags) for f in factors], axis=1).astype(ml_dtypes.bfloat16)


def factor_firsts():
    return [int(f) for f in np.concatenate([[0], np.cumsum([d + 1 for d in poly_degrees])])]


def down_factors(lags, lanes):
    bands = np.stack([banded(f, lags) for f in factor_table()])
    return np.pad(bands, ((0, 0), (0, 0), (0, lanes - lags.shape[1]))).astype(ml_dtypes.bfloat16)


def lane_packing():
    pack = np.zeros((TS // RIM, TS, TS))
    for g in range(TS // RIM):
        for r in range(RIM):
            pack[g, r, g * RIM + r] = 1.0
    return pack.reshape(-1, TS).astype(ml_dtypes.bfloat16)


def fold_weights(coeff_ref, yh, down_ref, out_ref):
    firsts = factor_firsts()
    k = 0
    for h, (s, p) in enumerate(across_pairs()):
        count = poly_degrees[s] + 1 - p
        factors = [down_ref[firsts[s] + q].astype(jnp.float32) for q in range(count)]
        terms = [
            sum(coeff_ref[k + q, m] * factors[q] for q in range(count))
            for m in range(len(poly_powers))
        ]
        k += count
        where = slice(h * TS, (h + 1) * TS)
        out_ref[0, :, where] = (terms[0] + yh * (terms[2] + yh * terms[5])).astype(jnp.bfloat16)
        out_ref[1, :, where] = (terms[1] + yh * terms[4]).astype(jnp.bfloat16)
        out_ref[2, :, where] = terms[3].astype(jnp.bfloat16)


def gather_kernel(
    owners,
    amps,
    owner,
    patch,
    row_shift,
    col_shift,
    coeff_ref,
    patches_ref,
    down_ref,
    rim_down_ref,
    pack_ref,
    template_ref,
    top_ref,
    low_ref,
    weight_ref,
    rim_weight_ref,
    store,
    rim_wide,
    top_land,
    low_land,
    direct_send,
    direct_recv,
    pass_send,
    pass_recv,
    own_send,
    own_recv,
    rim_send,
    rim_recv,
):
    mine = lax.axis_index("ccd")
    amp = lax.axis_index("amp")
    core = lax.rem(mine, 2)
    chip = lax.div(mine, 2)
    sibling = chip * 2 + 1 - core
    chips = owners // 2
    half = patches_ref.shape[0] // 2

    barrier = pltpu.get_barrier_semaphore()
    for step in range(1, owners):
        pl.semaphore_signal(
            barrier,
            inc=1,
            device_id=(lax.rem(mine + step, owners), amp),
            device_id_type=pl.DeviceIdType.MESH,
        )
    for step in (1, amps - 1):
        pl.semaphore_signal(
            barrier,
            inc=1,
            device_id=(mine, lax.rem(amp + step, amps)),
            device_id_type=pl.DeviceIdType.MESH,
        )
    store[mine] = patches_ref[...].astype(jnp.bfloat16)
    pl.semaphore_wait(barrier, owners - 1 + 2)

    def halves(of, which):
        return store.at[of, pl.ds(which * half, half)]

    def move(ref, send_sem, recv_sem, device):
        return pltpu.make_async_remote_copy(
            src_ref=ref,
            dst_ref=ref,
            send_sem=send_sem,
            recv_sem=recv_sem,
            device_id=device,
            device_id_type=pl.DeviceIdType.MESH,
        )

    sent = []
    for step in range(1, chips):
        target = lax.rem(chip + step, chips) * 2
        for j in range(2):
            copy = move(
                halves(mine, j),
                direct_send.at[step - 1, j],
                direct_recv.at[step - 1, core],
                (target + j, amp),
            )
            copy.start()
            sent.append(copy)
    own = move(store.at[mine], own_send, own_recv, (sibling, amp))
    own.start()

    rows = down_ref.shape[1]
    row = amp * rows + lax.broadcasted_iota(jnp.int32, (rows, 1), 0)
    yh = (2.0 * row.astype(jnp.float32) + 1.0) / (amps * rows) - 1.0
    fold_weights(coeff_ref, yh, down_ref, weight_ref)
    edge = lax.broadcasted_iota(jnp.int32, (2 * RIM, 1), 0)
    edge = amp * rows + jnp.where(edge < RIM, edge, rows - 2 * RIM + edge)
    yh = (2.0 * edge.astype(jnp.float32) + 1.0) / (amps * rows) - 1.0
    fold_weights(coeff_ref, yh, rim_down_ref, rim_wide)
    wide = rim_wide[...].reshape(3 * 2 * RIM, rim_wide.shape[2])
    group = pack_ref.shape[0]
    for g in range(rim_weight_ref.shape[2] // TS):
        part = wide[:, g * group : (g + 1) * group]
        packed = jnp.dot(part, pack_ref[: part.shape[1]], preferred_element_type=jnp.float32)
        rim_weight_ref[:, :, g * TS : (g + 1) * TS] = packed.astype(jnp.bfloat16).reshape(
            3, 2 * RIM, TS
        )

    for step in range(1, chips):
        source = lax.rem(chip + chips - step, chips) * 2
        for k in range(2):
            arrived = halves(source + k, core)
            move(
                arrived, direct_send.at[step - 1, k], direct_recv.at[step - 1, k], (sibling, amp)
            ).wait_recv()
            onward = move(
                arrived, pass_send.at[step - 1, k], pass_recv.at[step - 1, k], (sibling, amp)
            )
            onward.start()
            sent.append(onward)
    move(store.at[sibling], own_send, own_recv, (sibling, amp)).wait_recv()
    for step in range(1, chips):
        source = lax.rem(chip + chips - step, chips) * 2
        for k in range(2):
            move(
                halves(source + k, 1 - core),
                pass_send.at[step - 1, k],
                pass_recv.at[step - 1, k],
                (sibling, amp),
            ).wait_recv()

    row_lag = lax.broadcasted_iota(jnp.int32, (TS, 2 * TS), 1) - lax.broadcasted_iota(
        jnp.int32, (TS, 2 * TS), 0
    )
    col_lag = lax.broadcasted_iota(jnp.int32, (2 * TS, 2 * TS), 0) - lax.broadcasted_iota(
        jnp.int32, (2 * TS, 2 * TS), 1
    )
    column = lax.broadcasted_iota(jnp.int32, (2 * TS, 2 * TS), 1)
    held = (column >= TS // 2) & (column < TS // 2 + TS)
    col_lag = jnp.where(held, col_lag + TS // 2, -1)
    tiles = owner.shape[0]
    per_step = 8

    def cut(step, before):
        for j in range(per_step):
            t = step * per_step + j
            pick_rows = (row_lag == row_shift[t]).astype(jnp.float32).astype(jnp.bfloat16)
            pick_cols = (col_lag == col_shift[t]).astype(jnp.float32).astype(jnp.bfloat16)
            picked = jnp.dot(
                pick_rows, store[owner[t], patch[t]], preferred_element_type=jnp.float32
            )
            moved = jnp.dot(
                picked.astype(jnp.bfloat16), pick_cols, preferred_element_type=jnp.float32
            )
            first = pl.multiple_of(t * TS, TS)
            template_ref[:, pl.ds(first, TS)] = (before + moved[:, :TS]).astype(jnp.bfloat16)
            before = moved[:, TS:]
        return before

    last = lax.fori_loop(0, tiles // per_step, cut, jnp.zeros((TS, TS), jnp.float32))
    template_ref[:, tiles * TS :] = last.astype(jnp.bfloat16)

    def rim_copy(source, landing, which, step):
        return pltpu.make_async_remote_copy(
            src_ref=source,
            dst_ref=landing,
            send_sem=rim_send.at[which],
            recv_sem=rim_recv.at[which],
            device_id=(mine, lax.rem(amp + step, amps)),
            device_id_type=pl.DeviceIdType.MESH,
        )

    onto_next = rim_copy(template_ref.at[pl.ds(rows - RIM, RIM)], top_land, 0, 1)
    onto_previous = rim_copy(template_ref.at[pl.ds(0, RIM)], low_land, 1, amps - 1)
    onto_next.start()
    onto_previous.start()
    own.wait_send()
    for copy in sent:
        copy.wait_send()
    onto_next.wait()
    onto_previous.wait()
    top_ref[...] = jnp.where(amp > 0, top_land[...], jnp.zeros_like(top_land))
    low_ref[...] = jnp.where(amp < amps - 1, low_land[...], jnp.zeros_like(low_land))


def gather_and_cut(ids, coeffs, patches, down, rim_down, pack):
    owners, amps = lax.axis_size("ccd"), lax.axis_size("amp")
    tiles = ids[0].shape[0]
    count, rows, lanes = down.shape
    width = (tiles + 1) * TS
    rim_lanes = -(-count * RIM // TS) * TS
    smem = pl.BlockSpec(memory_space=pltpu.SMEM)
    vmem = pl.BlockSpec(memory_space=pltpu.VMEM)
    chips = owners // 2
    dma = pltpu.SemaphoreType.DMA
    return pl.pallas_call(
        functools.partial(gather_kernel, owners, amps),
        in_specs=[smem] * 5 + [vmem] * 4,
        out_specs=[vmem] * 5,
        out_shape=[
            jax.ShapeDtypeStruct((rows, width), jnp.bfloat16),
            jax.ShapeDtypeStruct((RIM, width), jnp.bfloat16),
            jax.ShapeDtypeStruct((RIM, width), jnp.bfloat16),
            jax.ShapeDtypeStruct((3, rows, count * TS), jnp.bfloat16),
            jax.ShapeDtypeStruct((3, 2 * RIM, rim_lanes), jnp.bfloat16),
        ],
        scratch_shapes=[
            pltpu.VMEM((owners,) + patches.shape, jnp.bfloat16),
            pltpu.VMEM((3, 2 * RIM, count * TS), jnp.bfloat16),
            pltpu.VMEM((RIM, width), jnp.bfloat16),
            pltpu.VMEM((RIM, width), jnp.bfloat16),
            dma((chips - 1, 2)),
            dma((chips - 1, 2)),
            dma((chips - 1, 2)),
            dma((chips - 1, 2)),
            dma(()),
            dma(()),
            dma((2,)),
            dma((2,)),
        ],
        compiler_params=pltpu.CompilerParams(
            collective_id=0, has_side_effects=True, vmem_limit_bytes=VMEM_BYTES
        ),
        cost_estimate=pl.CostEstimate(
            flops=tiles * 2 * TS * 8 * TS * TS, bytes_accessed=6 * 2**20, transcendentals=0
        ),
    )(*ids, coeffs, patches, down, rim_down, pack)


def apply_factors(windows, across_ref, weights, spread, columns, first_column):
    rows = windows[0].shape[0]
    stacked = jnp.concatenate(windows, axis=0)
    for pair in range(across_ref.shape[1] // WINDOW):
        result = jnp.dot(
            stacked,
            across_ref[:, pair * WINDOW : (pair + 1) * WINDOW],
            preferred_element_type=jnp.float32,
        ).astype(jnp.bfloat16)
        for b in range(len(windows)):
            for half in range(2):
                h = 2 * pair + half
                spread[h * rows : (h + 1) * rows, b * TS : (b + 1) * TS] = result[
                    b * rows : (b + 1) * rows, half * TS : (half + 1) * TS
                ]
    filled = across_ref.shape[1] // TS * rows
    if filled < spread.shape[0]:
        spread[filled:, :] = jnp.zeros((spread.shape[0] - filled, spread.shape[1]), spread.dtype)
    folded = jnp.dot(weights, spread[...], preferred_element_type=jnp.float32)
    out_rows = weights.shape[0] // 3
    width = len(windows) * TS
    position = first_column + lax.broadcasted_iota(jnp.int32, (1, width), 1)
    xh = (2.0 * position.astype(jnp.float32) + 1.0) / columns - 1.0
    return folded[:out_rows] + xh * (
        folded[out_rows : 2 * out_rows] + xh * folded[2 * out_rows :]
    )


def centre_kernel(columns, template_ref, across_ref, weight_ref, science_ref, out_ref, spread):
    width = out_ref.shape[1]
    first = pl.program_id(0) * width
    windows = [
        template_ref[:, pl.ds(pl.multiple_of(first + b * TS, TS), WINDOW)]
        for b in range(width // TS)
    ]
    weights = weight_ref[...].reshape(-1, weight_ref.shape[2])
    psf = apply_factors(windows, across_ref, weights, spread, columns, first)
    out_ref[...] = science_ref[...] - psf


def centre(template, across, weights, science, width):
    rows, columns = science.shape
    return pl.pallas_call(
        functools.partial(centre_kernel, columns),
        grid=(columns // width,),
        in_specs=[
            pl.BlockSpec(template.shape, lambda i: (0, 0)),
            pl.BlockSpec(across.shape, lambda i: (0, 0)),
            pl.BlockSpec(weights.shape, lambda i: (0, 0, 0)),
            pl.BlockSpec((rows, width), lambda i: (0, i)),
        ],
        out_specs=pl.BlockSpec((rows, width), lambda i: (0, i)),
        out_shape=jax.ShapeDtypeStruct(science.shape, jnp.float32),
        scratch_shapes=[pltpu.VMEM((weights.shape[2], width), jnp.bfloat16)],
        compiler_params=pltpu.CompilerParams(vmem_limit_bytes=VMEM_BYTES),
        cost_estimate=pl.CostEstimate(
            flops=2 * columns * weights.shape[2] * (3 * rows + WINDOW),
            bytes_accessed=8 * rows * columns + 4 * 2**20,
            transcendentals=0,
        ),
    )(template, across, weights, science)


def rim_kernel(columns, top_ref, low_ref, across_ref, weight_ref, held_ref, out_ref, spread):
    width = out_ref.shape[1]
    first = pl.program_id(1) * width
    is_top = pl.program_id(0) == 0
    windows = []
    for b in range(width // TS):
        where = pl.ds(pl.multiple_of(first + b * TS, TS), WINDOW)
        windows.append(jnp.where(is_top, top_ref[:, where], low_ref[:, where]))
    weights = weight_ref[...].reshape(-1, weight_ref.shape[2])
    psf = apply_factors(windows, across_ref, weights, spread, columns, first)
    out_ref[...] = held_ref[...] - psf


def rims(top, low, across, weights, held, width):
    rows, columns = held.shape
    last = rows // RIM - 1
    return pl.pallas_call(
        functools.partial(rim_kernel, columns),
        grid=(2, columns // width),
        in_specs=[
            pl.BlockSpec(top.shape, lambda v, i: (0, 0)),
            pl.BlockSpec(low.shape, lambda v, i: (0, 0)),
            pl.BlockSpec(across.shape, lambda v, i: (0, 0)),
            pl.BlockSpec((3, RIM, weights.shape[2]), lambda v, i: (0, v, 0)),
            pl.BlockSpec((RIM, width), lambda v, i: (v * last, i)),
        ],
        out_specs=pl.BlockSpec((RIM, width), lambda v, i: (v * last, i)),
        out_shape=jax.ShapeDtypeStruct(held.shape, jnp.float32),
        scratch_shapes=[pltpu.VMEM((weights.shape[2], width), jnp.bfloat16)],
        input_output_aliases={4: 0},
        compiler_params=pltpu.CompilerParams(vmem_limit_bytes=VMEM_BYTES),
        cost_estimate=pl.CostEstimate(
            flops=4 * columns * weights.shape[2] * (3 * RIM + WINDOW),
            bytes_accessed=2**20,
            transcendentals=0,
        ),
    )(top, low, across, weights, held)


def per_device(science, patches, coeffs, tile_owner, tile_patch, tile_offset):
    ccd_id = lax.axis_index("ccd")
    amp_id = lax.axis_index("amp")
    strip_rows, columns = science.shape[1:]

    ids = (
        tile_owner[ccd_id, amp_id, :, 0],
        tile_patch[ccd_id, amp_id],
        tile_offset[ccd_id, amp_id, :, 0],
        tile_offset[ccd_id, amp_id, :, 1],
    )
    across = jnp.asarray(across_matrix())
    row = np.arange(strip_rows)
    down = down_factors(row[None, :] - row[:, None], strip_rows)
    rim_row = np.arange(RIM)
    top_lags = (rim_row[None, :] - RIM) - rim_row[:, None]
    low_lags = (rim_row[None, :] + RIM) - rim_row[:, None]
    rim_down = down_factors(np.concatenate([top_lags, low_lags], axis=0), TS)
    template, top, low, centre_weights, rim_weights = gather_and_cut(
        ids,
        coeffs[0],
        patches[0, 0],
        jnp.asarray(down),
        jnp.asarray(rim_down),
        jnp.asarray(lane_packing()),
    )
    inner = centre(template, across, centre_weights, science[0], 8 * TS)
    return rims(top, low, across, rim_weights, inner, 16 * TS)[None]


def solution(mesh):
    placed = (
        P("ccd", "amp", None),
        P("ccd", "amp", None, None, None),
        P("ccd", None, None),
        P(),
        P(),
        P(),
    )
    return jax.shard_map(
        per_device, mesh=mesh, in_specs=placed, out_specs=P("ccd", "amp", None), check_vma=False
    )
```

time: 82.8 us -> 64.2 us (0.78)
  Pallas kernels: 23 us -> 57.3 us
  waiting for transfers between devices: 33.2 us -> 0 us
  between operations: 13.6 us -> 0.03 us
  starting transfers between devices: 4.72 us -> 0 us
  other arithmetic: 2.34 us -> 0 us
  local copies, waits for them, and re-layouts: 4.65 us -> 6.48 us
  matrix products: 1.03 us -> 0 us
    pallas_call x3 -> x1, Pallas kernels: 6 us -> 40.2 us  [gather_and_cut(): pl.pallas_call(functools.partial(gather_kernel, owners, amps), in_specs=[...]
    all_gather x1 -> x0, waiting for transfers between devices: 33.2 us -> none  [per_device(): lax.all_gather(patches.astype(jnp.bfloat16), 'ccd', axis=0, tiled=True)]
    ppermute x2 -> x0, starting transfers between devices: 4.69 us -> none  [the longest x1 3.4 us: per_device(): top = lax.ppermute(template[-RIM:], 'amp', forward)]
    convert_element_type x1 -> x0, other arithmetic: 2.23 us -> none  [per_device(): patches.astype(jnp.bfloat16)]
    unnamed x20 -> x15, local copies, waits for them, and re-layouts: 3.38 us -> 5.58 us
    dot_general x1 -> x0, matrix products: 1.03 us -> none  [per_device(): jnp.einsum('qhk,km->mqh', select, coeffs[0], precision=lax.Precision.HIGH...]
  transfers between devices with their start and end apart: 3 -> 0, of which waited for: 1 -> 0; matrix products, arithmetic and copies ran while one was open for 3% -> 0% of each run, Pallas kernels for 19% -> 0%
where the time goes in v2:
time: 64.2 us; the launch traced here: 63.8 us
  Pallas kernels  57.3 us (89%)
  local copies, waits for them, and re-layouts  6.48 us (10%)
    pallas_call x1, Pallas kernels, gather_and_cut(): pl.pallas_call(functools.partial(gather_kernel, owners, amps), in_specs=[...  40.2 us
    pallas_call x1, Pallas kernels, centre(): pl.pallas_call(functools.partial(centre_kernel, columns), grid=(columns /...  12.4 us
    unnamed x15, local copies, waits for them, and re-layouts  5.58 us
    pallas_call x1, Pallas kernels, rims(): pl.pallas_call(functools.partial(rim_kernel, columns), grid=(2, columns /...  4.7 us

profile of v2, /device:TPU:0, one launch (start us, length us, event | category | flops | bytes accessed | tf_op | source)
XLA Modules:
  0.0 63.8 jit_solution(1608723856945913245)
XLA Ops:
  0.0 0.0 copy-start
  0.0 0.0 copy-start.1
  0.0 0.0 copy-start.2
  0.0 0.7 %copy-done = s32[8,4,32]{2,1,0:T(4,128)S(1)} copy-done((s32[8,4,32]{2,1,0:T(4,128)S(1)}, s32[8,4,32]{2,1,0:T(4,128)}, u32[]{:S(2)}) %copy-start) | copy-done | bytes 4120
  0.7 0.9 %fusion.3 = (s32[32]{0:T(128)S(1)}, s32[32]{0:T(128)S(1)}, s32[32]{0:T(128)S(1)}) fusion(s32[8,4,32,2]{2,3,1,0:T(2,128)} %param.15, s32[]{:T(128)S(6)} %select_n.4, s32[]{:T(128)S(6)} %select_n.5, s32[8,4,32,1]{2,3,1,0:T(1,128)} %param.13), kind=kLoop, calls=%fused_computation.7 | loop fusion | bytes 776 | tf_op jit(solution)/shard_map/squeeze | solution.py:416
  1.6 0.8 %copy.12 = f32[1,40,6]{2,1,0:T(8,128)S(1)} copy(f32[1,40,6]{1,0,2:T(1,128)} %param.12) | data formatting | bytes 1920 | tf_op args[2]
  2.4 0.0 copy-start.3
  2.4 1.2 %copy-done.3 = f32[1,1,4,256,256]{4,3,2,1,0:T(8,128)S(1)} copy-done((f32[1,1,4,256,256]{4,3,2,1,0:T(8,128)S(1)}, f32[1,1,4,256,256]{4,3,2,1,0:T(8,128)}, u32[]{:S(2)}) %copy-start.3) | copy-done | bytes 1048600
  3.6 0.0 copy-start.4
  3.6 1.0 %copy-done.4 = bf16[14,128,128]{2,1,0:T(8,128)(2,1)S(1)} copy-done((bf16[14,128,128]{2,1,0:T(8,128)(2,1)S(1)}, bf16[14,128,128]{2,1,0:T(8,128)(2,1)}, u32[]{:S(2)}) %copy-start.4) | copy-done | bytes 458776
  4.6 0.0 copy-start.5
  4.6 0.9 %copy-done.5 = bf16[1024,128]{1,0:T(8,128)(2,1)S(1)} copy-done((bf16[1024,128]{1,0:T(8,128)(2,1)S(1)}, bf16[1024,128]{1,0:T(8,128)(2,1)}, u32[]{:S(2)}) %copy-start.5) | copy-done | bytes 262168
  5.6 0.0 copy-start.6
  5.6 0.9 %copy-done.6 = bf16[14,32,128]{2,1,0:T(8,128)(2,1)S(1)} copy-done((bf16[14,32,128]{2,1,0:T(8,128)(2,1)S(1)}, bf16[14,32,128]{2,1,0:T(8,128)(2,1)}, u32[]{:S(2)}) %copy-start.6) | copy-done | bytes 114712
  6.5 40.2 %shard_map.100 = (bf16[128,4224]{1,0:T(8,128)(2,1)S(1)}, bf16[16,4224]{1,0:T(8,128)(2,1)S(1)}, bf16[16,4224]{1,0:T(8,128)(2,1)S(1)}, bf16[3,128,1792]{2,1,0:T(8,128)(2,1)S(1)}, bf16[3,32,256]{2,1,0:T(8,128)(2,1)S(1)}) custom-call(s32[32]{0:T(128)S(1)} %get-tuple-element.17.owner, s32[32]{0:T(128)S(1)} %fusion.1.patch, s32[32]{0:T(128)S(1)} %get-tuple-element.16.row_shift, ...), custom_call_target="tpu_custom_call" | custom-call | flops 1073741824 | bytes 6291456 | tf_op jit(solution)/shard_map/pallas_call | solution.py:271
  46.7 0.0 copy-done.1
  46.7 0.0 copy-done.2
  46.8 12.4 %shard_map.101.held_ref = f32[128,4096]{1,0:T(8,128)} custom-call(bf16[128,4224]{1,0:T(8,128)(2,1)S(1)} %get-tuple-element.13.template_ref, bf16[256,1792]{1,0:T(8,128)(2,1)S(1)} %copy-done.1, bf16[3,128,1792]{2,1,0:T(8,128)(2,1)S(1)} %get-tuple-element.14.weight_ref, f32[128,4096]{1,0:T(8,128)S(1)} %bitcast.13), custom_call_target="tpu_custom_call" | custom-call | flops 9395240960 | bytes 8388608 | tf_op jit(solution)/shard_map/pallas_call | solution.py:347
  59.1 4.7 %shard_map.102 = f32[128,4096]{1,0:T(8,128)} custom-call(bf16[16,4224]{1,0:T(8,128)(2,1)S(1)} %get-tuple-element.10.top_ref, bf16[16,4224]{1,0:T(8,128)(2,1)S(1)} %get-tuple-element.11.low_ref, bf16[256,1792]{1,0:T(8,128)(2,1)S(1)} %copy-done.1, bf16[3,32,256]{2,1,0:T(8,128)(2,1)S(1)} %get-tuple-element.12.weight_ref, ...), custom_call_target="tpu_custom_call", output_to_operand_aliasing={{}: (4, {})} | custom-call | flops 1275068416 | bytes 1048576 | tf_op jit(solution)/shard_map/pallas_call | solution.py:384
  (1 shorter events, 0.0 us)
Async XLA Ops:
  0.0 0.7 %copy-start = (s32[8,4,32]{2,1,0:T(4,128)S(1)}, s32[8,4,32]{2,1,0:T(4,128)}, u32[]{:S(2)}) copy-start(s32[8,4,32]{2,1,0:T(4,128)} %param.14) | copy-start | bytes 12292
  0.0 46.7 %copy-start.1 = (bf16[256,1792]{1,0:T(8,128)(2,1)S(1)}, bf16[256,1792]{1,0:T(8,128)(2,1)}, u32[]{:S(2)}) copy-start(bf16[256,1792]{1,0:T(8,128)(2,1)} %constant.25.clone.across_ref) | copy-start | bytes 2752516
  0.0 46.7 %copy-start.2 = (f32[1,128,4096]{2,1,0:T(8,128)S(1)}, f32[1,128,4096]{2,1,0:T(8,128)}, u32[]{:S(2)}) copy-start(f32[1,128,4096]{2,1,0:T(8,128)} %param.10) | copy-start | bytes 6291460
  2.4 1.2 %copy-start.3 = (f32[1,1,4,256,256]{4,3,2,1,0:T(8,128)S(1)}, f32[1,1,4,256,256]{4,3,2,1,0:T(8,128)}, u32[]{:S(2)}) copy-start(f32[1,1,4,256,256]{4,3,2,1,0:T(8,128)} %param.11) | copy-start | bytes 3145732
  3.6 1.0 %copy-start.4 = (bf16[14,128,128]{2,1,0:T(8,128)(2,1)S(1)}, bf16[14,128,128]{2,1,0:T(8,128)(2,1)}, u32[]{:S(2)}) copy-start(bf16[14,128,128]{2,1,0:T(8,128)(2,1)} %constant.26.clone.down_ref) | copy-start | bytes 1376260
  4.6 0.9 %copy-start.5 = (bf16[1024,128]{1,0:T(8,128)(2,1)S(1)}, bf16[1024,128]{1,0:T(8,128)(2,1)}, u32[]{:S(2)}) copy-start(bf16[1024,128]{1,0:T(8,128)(2,1)} %constant.28.clone.pack_ref) | copy-start | bytes 786436
  5.6 0.9 %copy-start.6 = (bf16[14,32,128]{2,1,0:T(8,128)(2,1)S(1)}, bf16[14,32,128]{2,1,0:T(8,128)(2,1)}, u32[]{:S(2)}) copy-start(bf16[14,32,128]{2,1,0:T(8,128)(2,1)} %constant.27.clone.rim_down_ref) | copy-start | bytes 344068

commit v3 on v2

v3 whole, which is shorter than its diff:
```python
import functools

import jax
import jax.numpy as jnp
import ml_dtypes
import numpy as np
from jax import lax
from jax.experimental import pallas as pl
from jax.experimental.pallas import tpu as pltpu
from jax.sharding import PartitionSpec as P

TS = 128
HALF = 10
RIM = 16
WINDOW = 2 * TS
VMEM_BYTES = 60 * 2**20

gauss_widths = (1.0, 2.0, 4.0)
poly_degrees = (4, 4, 3)
poly_powers = ((0, 0), (1, 0), (0, 1), (2, 0), (1, 1), (0, 2))


def factor_table():
    offsets = np.arange(-HALF, HALF + 1).astype(np.float64)
    shapes = []
    for sigma_px, degree in zip(gauss_widths, poly_degrees):
        for exponent in range(degree + 1):
            profile = np.exp(-offsets * offsets / (2.0 * sigma_px * sigma_px))
            profile = profile * (offsets / HALF) ** exponent
            shapes.append(profile / np.sum(np.abs(profile)))
    return np.stack(shapes).astype(np.float32).astype(ml_dtypes.bfloat16).astype(np.float32)


def across_pairs():
    return [(s, p) for s, degree in enumerate(poly_degrees) for p in range(degree + 1)]


def banded(taps, lags):
    inside = np.abs(lags) <= HALF
    return np.where(inside, taps[np.clip(lags + HALF, 0, 2 * HALF)], 0.0)


def across_matrix():
    factors = factor_table()
    lags = np.arange(WINDOW)[:, None] - TS // 2 - np.arange(TS)[None, :]
    return np.concatenate([banded(f, lags) for f in factors], axis=1).astype(ml_dtypes.bfloat16)


def factor_firsts():
    return [int(f) for f in np.concatenate([[0], np.cumsum([d + 1 for d in poly_degrees])])]


def down_factors(lags, lanes):
    bands = np.stack([banded(f, lags) for f in factor_table()])
    return np.pad(bands, ((0, 0), (0, 0), (0, lanes - lags.shape[1]))).astype(ml_dtypes.bfloat16)


def lane_packing():
    pack = np.zeros((TS // RIM, TS, TS))
    for g in range(TS // RIM):
        for r in range(RIM):
            pack[g, r, g * RIM + r] = 1.0
    return pack.reshape(-1, TS).astype(ml_dtypes.bfloat16)


def fold_weights(coeff_ref, yh, down_ref, out_ref):
    firsts = factor_firsts()
    k = 0
    for h, (s, p) in enumerate(across_pairs()):
        count = poly_degrees[s] + 1 - p
        factors = [down_ref[firsts[s] + q].astype(jnp.float32) for q in range(count)]
        terms = [
            sum(coeff_ref[m, 0, k + q] * factors[q] for q in range(count))
            for m in range(len(poly_powers))
        ]
        k += count
        where = slice(h * TS, (h + 1) * TS)
        out_ref[0, :, where] = (terms[0] + yh * (terms[2] + yh * terms[5])).astype(jnp.bfloat16)
        out_ref[1, :, where] = (terms[1] + yh * terms[4]).astype(jnp.bfloat16)
        out_ref[2, :, where] = terms[3].astype(jnp.bfloat16)


def gather_kernel(
    owners,
    amps,
    owner_hbm,
    patch_hbm,
    offset_hbm,
    coeff_hbm,
    patches_hbm,
    down_hbm,
    rim_down_hbm,
    pack_hbm,
    template_ref,
    top_ref,
    low_ref,
    weight_ref,
    rim_weight_ref,
    owner_ref,
    patch_ref,
    offset_ref,
    coeff_ref,
    patches_ref,
    down_ref,
    rim_down_ref,
    pack_ref,
    store,
    rim_wide,
    top_land,
    low_land,
    local_sem,
    direct_send,
    direct_recv,
    relay_send,
    relay_recv,
    pass_send,
    pass_recv,
    own_send,
    own_recv,
    rim_send,
    rim_recv,
):
    mine = lax.axis_index("ccd")
    amp = lax.axis_index("amp")
    core = lax.rem(mine, 2)
    chip = lax.div(mine, 2)
    sibling = chip * 2 + 1 - core
    chips = owners // 2
    half = patches_ref.shape[0] // 2

    fetch_patches = pltpu.make_async_copy(patches_hbm.at[0, 0], patches_ref, local_sem.at[0])
    fetch_patches.start()
    barrier = pltpu.get_barrier_semaphore()
    for step in range(1, owners):
        pl.semaphore_signal(
            barrier,
            inc=1,
            device_id=(lax.rem(mine + step, owners), amp),
            device_id_type=pl.DeviceIdType.MESH,
        )
    for step in (1, amps - 1):
        pl.semaphore_signal(
            barrier,
            inc=1,
            device_id=(mine, lax.rem(amp + step, amps)),
            device_id_type=pl.DeviceIdType.MESH,
        )
    fetches = [
        pltpu.make_async_copy(source, target, local_sem.at[1 + i])
        for i, (source, target) in enumerate(
            (
                (coeff_hbm, coeff_ref),
                (down_hbm, down_ref),
                (rim_down_hbm, rim_down_ref),
                (pack_hbm, pack_ref),
                (owner_hbm.at[mine, amp], owner_ref),
                (patch_hbm.at[mine], patch_ref),
                (offset_hbm.at[mine, amp], offset_ref),
            )
        )
    ]
    for fetch in fetches:
        fetch.start()
    fetch_patches.wait()
    store[mine] = patches_ref[...].astype(jnp.bfloat16)
    pl.semaphore_wait(barrier, owners - 1 + 2)

    def halves(of, which):
        return store.at[of, pl.ds(which * half, half)]

    def move(ref, send_sem, recv_sem, device):
        return pltpu.make_async_remote_copy(
            src_ref=ref,
            dst_ref=ref,
            send_sem=send_sem,
            recv_sem=recv_sem,
            device_id=device,
            device_id_type=pl.DeviceIdType.MESH,
        )

    if chips == 4:
        beside = chip + 1 - 2 * lax.rem(chip, 2)
        above = lax.rem(chip + 2, 4)
        across_both = lax.rem(beside + 2, 4)
        exchanges = [(beside, beside), (above, above)]
    else:
        exchanges = [
            (lax.rem(chip + step, chips), lax.rem(chip + chips - step, chips))
            for step in range(1, chips)
        ]

    sent = []
    for i, (target, _) in enumerate(exchanges):
        for j in range(2):
            copy = move(
                halves(mine, j),
                direct_send.at[i, j],
                direct_recv.at[i, core],
                (target * 2 + j, amp),
            )
            copy.start()
            sent.append(copy)
    own = move(store.at[mine], own_send, own_recv, (sibling, amp))
    own.start()

    for fetch in fetches:
        fetch.wait()
    rows = down_ref.shape[1]
    row = amp * rows + lax.broadcasted_iota(jnp.int32, (rows, 1), 0)
    yh = (2.0 * row.astype(jnp.float32) + 1.0) / (amps * rows) - 1.0
    fold_weights(coeff_ref, yh, down_ref, weight_ref)
    edge = lax.broadcasted_iota(jnp.int32, (2 * RIM, 1), 0)
    edge = amp * rows + jnp.where(edge < RIM, edge, rows - 2 * RIM + edge)
    yh = (2.0 * edge.astype(jnp.float32) + 1.0) / (amps * rows) - 1.0
    fold_weights(coeff_ref, yh, rim_down_ref, rim_wide)
    wide = rim_wide[...].reshape(3 * 2 * RIM, rim_wide.shape[2])
    group = pack_ref.shape[0]
    for g in range(rim_weight_ref.shape[2] // TS):
        part = wide[:, g * group : (g + 1) * group]
        packed = jnp.dot(part, pack_ref[: part.shape[1]], preferred_element_type=jnp.float32)
        rim_weight_ref[:, :, g * TS : (g + 1) * TS] = packed.astype(jnp.bfloat16).reshape(
            3, 2 * RIM, TS
        )

    def pass_on(i, k, source):
        onward = move(
            halves(source * 2 + k, core), pass_send.at[i, k], pass_recv.at[i, k], (sibling, amp)
        )
        onward.start()
        sent.append(onward)

    def relay(which, source, target):
        return move(
            halves(source * 2 + which, core),
            relay_send.at[which],
            relay_recv.at[which],
            (target * 2 + core, amp),
        )

    sources = [source for _, source in exchanges]
    order = [(i, k) for k in range(2) for i in range(len(exchanges))]
    if chips == 4:
        order = [(1, 0), (0, 1), (0, 0), (1, 1)]
    for i, k in order:
        move(
            halves(sources[i] * 2 + k, core),
            direct_send.at[i, k],
            direct_recv.at[i, k],
            (sibling, amp),
        ).wait_recv()
        if chips == 4 and i != k:
            onward = relay(k, sources[i], sources[1 - i])
            onward.start()
            sent.append(onward)
        pass_on(i, k, sources[i])
    if chips == 4:
        for k in range(2):
            relay(k, across_both, beside).wait_recv()
            pass_on(2, k, across_both)
        sources = sources + [across_both]
    move(store.at[sibling], own_send, own_recv, (sibling, amp)).wait_recv()
    for i, source in enumerate(sources):
        for k in range(2):
            move(
                halves(source * 2 + k, 1 - core),
                pass_send.at[i, k],
                pass_recv.at[i, k],
                (sibling, amp),
            ).wait_recv()

    row_lag = lax.broadcasted_iota(jnp.int32, (TS, 2 * TS), 1) - lax.broadcasted_iota(
        jnp.int32, (TS, 2 * TS), 0
    )
    col_lag = lax.broadcasted_iota(jnp.int32, (2 * TS, 2 * TS), 0) - lax.broadcasted_iota(
        jnp.int32, (2 * TS, 2 * TS), 1
    )
    column = lax.broadcasted_iota(jnp.int32, (2 * TS, 2 * TS), 1)
    held = (column >= TS // 2) & (column < TS // 2 + TS)
    col_lag = jnp.where(held, col_lag + TS // 2, -1)
    tiles = owner_ref.shape[1]
    per_step = 8

    def cut(step, before):
        for j in range(per_step):
            t = step * per_step + j
            pick_rows = (row_lag == offset_ref[0, t]).astype(jnp.float32).astype(jnp.bfloat16)
            pick_cols = (col_lag == offset_ref[1, t]).astype(jnp.float32).astype(jnp.bfloat16)
            picked = jnp.dot(
                pick_rows, store[owner_ref[0, t], patch_ref[amp, t]], preferred_element_type=jnp.float32
            )
            moved = jnp.dot(
                picked.astype(jnp.bfloat16), pick_cols, preferred_element_type=jnp.float32
            )
            first = pl.multiple_of(t * TS, TS)
            template_ref[:, pl.ds(first, TS)] = (before + moved[:, :TS]).astype(jnp.bfloat16)
            before = moved[:, TS:]
        return before

    def rim_copies(part, where):
        return [
            pltpu.make_async_remote_copy(
                src_ref=template_ref.at[pl.ds(first, RIM), where],
                dst_ref=landing.at[:, where],
                send_sem=rim_send.at[part, which],
                recv_sem=rim_recv.at[part, which],
                device_id=(mine, lax.rem(amp + step, amps)),
                device_id_type=pl.DeviceIdType.MESH,
            )
            for which, (first, landing, step) in enumerate(
                ((rows - RIM, top_land, 1), (0, low_land, amps - 1))
            )
        ]

    steps = tiles // per_step
    early = steps // 2 * per_step * TS
    before = lax.fori_loop(0, steps // 2, cut, jnp.zeros((TS, TS), jnp.float32))
    rims = rim_copies(0, pl.ds(0, early))
    for copy in rims:
        copy.start()
    last = lax.fori_loop(steps // 2, steps, cut, before)
    template_ref[:, tiles * TS :] = last.astype(jnp.bfloat16)
    rest = rim_copies(1, pl.ds(early, (tiles + 1) * TS - early))
    for copy in rest:
        copy.start()
    own.wait_send()
    for copy in sent:
        copy.wait_send()
    for copy in rims + rest:
        copy.wait()
    top_ref[...] = jnp.where(amp > 0, top_land[...], jnp.zeros_like(top_land))
    low_ref[...] = jnp.where(amp < amps - 1, low_land[...], jnp.zeros_like(low_land))


def gather_and_cut(owner, patch, offset, coeffs, patches, down, rim_down, pack):
    owners, amps = lax.axis_size("ccd"), lax.axis_size("amp")
    tiles = patch.shape[2]
    count, rows, lanes = down.shape
    width = (tiles + 1) * TS
    rim_lanes = -(-count * RIM // TS) * TS
    vmem = pl.BlockSpec(memory_space=pltpu.VMEM)
    chips = owners // 2
    dma = pltpu.SemaphoreType.DMA
    return pl.pallas_call(
        functools.partial(gather_kernel, owners, amps),
        in_specs=[pl.BlockSpec(memory_space=pl.ANY)] * 8,
        out_specs=[vmem] * 5,
        out_shape=[
            jax.ShapeDtypeStruct((rows, width), jnp.bfloat16),
            jax.ShapeDtypeStruct((RIM, width), jnp.bfloat16),
            jax.ShapeDtypeStruct((RIM, width), jnp.bfloat16),
            jax.ShapeDtypeStruct((3, rows, count * TS), jnp.bfloat16),
            jax.ShapeDtypeStruct((3, 2 * RIM, rim_lanes), jnp.bfloat16),
        ],
        scratch_shapes=[
            pltpu.SMEM(owner.shape[2:], jnp.int32),
            pltpu.SMEM(patch.shape[1:], jnp.int32),
            pltpu.SMEM(offset.shape[2:], jnp.int32),
            pltpu.SMEM(coeffs.shape, jnp.float32),
            pltpu.VMEM(patches.shape[2:], jnp.float32),
            pltpu.VMEM(down.shape, jnp.bfloat16),
            pltpu.VMEM(rim_down.shape, jnp.bfloat16),
            pltpu.VMEM(pack.shape, jnp.bfloat16),
            pltpu.VMEM((owners,) + patches.shape[2:], jnp.bfloat16),
            pltpu.VMEM((3, 2 * RIM, count * TS), jnp.bfloat16),
            pltpu.VMEM((RIM, width), jnp.bfloat16),
            pltpu.VMEM((RIM, width), jnp.bfloat16),
            dma((8,)),
            dma((chips - 1, 2)),
            dma((chips - 1, 2)),
            dma((2,)),
            dma((2,)),
            dma((chips - 1, 2)),
            dma((chips - 1, 2)),
            dma(()),
            dma(()),
            dma((2, 2)),
            dma((2, 2)),
        ],
        compiler_params=pltpu.CompilerParams(
            collective_id=0, has_side_effects=True, vmem_limit_bytes=VMEM_BYTES
        ),
        cost_estimate=pl.CostEstimate(
            flops=tiles * 2 * TS * 8 * TS * TS, bytes_accessed=6 * 2**20, transcendentals=0
        ),
    )(owner, patch, offset, coeffs, patches, down, rim_down, pack)


def polynomial(folded, xh):
    rows = folded.shape[0] // 3
    return folded[:rows] + xh * (folded[rows : 2 * rows] + xh * folded[2 * rows :])


def filter_kernel(
    columns,
    template_ref,
    top_ref,
    low_ref,
    across_ref,
    weight_ref,
    rim_weight_ref,
    science_ref,
    out_ref,
    spread,
    rim_spread,
):
    rows, width = out_ref.shape
    blocks = width // TS
    first = pl.program_id(0) * width
    starts = [pl.multiple_of(first + b * TS, TS) for b in range(blocks)]
    parts = [(template_ref, spread, rows), (top_ref, rim_spread.at[0], RIM)]
    parts.append((low_ref, rim_spread.at[1], RIM))
    stacked = jnp.concatenate(
        [ref[:, pl.ds(start, WINDOW)] for ref, _, _ in parts for start in starts], axis=0
    )
    for pair in range(across_ref.shape[1] // WINDOW):
        result = jnp.dot(
            stacked,
            across_ref[:, pair * WINDOW : (pair + 1) * WINDOW],
            preferred_element_type=jnp.float32,
        ).astype(jnp.bfloat16)
        begin = 0
        for _, target, height in parts:
            for b in range(blocks):
                for side in range(2):
                    h = 2 * pair + side
                    target[h * height : (h + 1) * height, b * TS : (b + 1) * TS] = result[
                        begin : begin + height, side * TS : (side + 1) * TS
                    ]
                begin += height
    filled = across_ref.shape[1] // TS * RIM
    if filled < rim_spread.shape[1]:
        unused = (2, rim_spread.shape[1] - filled, width)
        rim_spread[:, filled:, :] = jnp.zeros(unused, rim_spread.dtype)
    position = first + lax.broadcasted_iota(jnp.int32, (1, width), 1)
    xh = (2.0 * position.astype(jnp.float32) + 1.0) / columns - 1.0
    weights = weight_ref[...].reshape(3 * rows, weight_ref.shape[2])
    folded = jnp.dot(weights, spread[...], preferred_element_type=jnp.float32)
    out_ref[...] = science_ref[...] - polynomial(folded, xh)
    for side, begin in enumerate((0, rows - RIM)):
        weights = rim_weight_ref[:, side * RIM : (side + 1) * RIM, :]
        weights = weights.reshape(3 * RIM, rim_weight_ref.shape[2])
        folded = jnp.dot(weights, rim_spread[side], preferred_element_type=jnp.float32)
        out_ref[begin : begin + RIM, :] -= polynomial(folded, xh)


def filter_strip(template, top, low, across, weights, rim_weights, science, width):
    rows, columns = science.shape

    def whole(array):
        return pl.BlockSpec(array.shape, lambda i: (0,) * array.ndim)

    constant = (template, top, low, across, weights, rim_weights)
    return pl.pallas_call(
        functools.partial(filter_kernel, columns),
        grid=(columns // width,),
        in_specs=[whole(x) for x in constant] + [pl.BlockSpec((rows, width), lambda i: (0, i))],
        out_specs=pl.BlockSpec((rows, width), lambda i: (0, i)),
        out_shape=jax.ShapeDtypeStruct(science.shape, jnp.float32),
        scratch_shapes=[
            pltpu.VMEM((weights.shape[2], width), jnp.bfloat16),
            pltpu.VMEM((2, rim_weights.shape[2], width), jnp.bfloat16),
        ],
        compiler_params=pltpu.CompilerParams(vmem_limit_bytes=VMEM_BYTES),
        cost_estimate=pl.CostEstimate(
            flops=2 * columns * weights.shape[2] * (3 * rows + WINDOW),
            bytes_accessed=8 * rows * columns + 4 * 2**20,
            transcendentals=0,
        ),
    )(*constant, science)


def per_device(science, patches, coeffs, tile_owner, tile_patch, tile_offset):
    strip_rows = science.shape[1]

    across = jnp.asarray(across_matrix())
    row = np.arange(strip_rows)
    down = down_factors(row[None, :] - row[:, None], strip_rows)
    rim_row = np.arange(RIM)
    top_lags = (rim_row[None, :] - RIM) - rim_row[:, None]
    low_lags = (rim_row[None, :] + RIM) - rim_row[:, None]
    rim_down = down_factors(np.concatenate([top_lags, low_lags], axis=0), TS)
    template, top, low, weights, rim_weights = gather_and_cut(
        jnp.transpose(tile_owner, (0, 1, 3, 2)),
        tile_patch,
        jnp.transpose(tile_offset, (0, 1, 3, 2)),
        jnp.transpose(coeffs, (2, 0, 1)),
        patches,
        jnp.asarray(down),
        jnp.asarray(rim_down),
        jnp.asarray(lane_packing()),
    )
    return filter_strip(
        template, top, low, across, weights, rim_weights, science[0], 8 * TS
    )[None]


def solution(mesh):
    placed = (
        P("ccd", "amp", None),
        P("ccd", "amp", None, None, None),
        P("ccd", None, None),
        P(),
        P(),
        P(),
    )
    return jax.shard_map(
        per_device, mesh=mesh, in_specs=placed, out_specs=P("ccd", "amp", None), check_vma=False
    )
```

time: 64.2 us -> 50.5 us (0.79)
  Pallas kernels: 57.3 us -> 50.4 us
  local copies, waits for them, and re-layouts: 6.48 us -> 0 us
    unnamed x15 -> x0, local copies, waits for them, and re-layouts: 5.58 us -> none
    pallas_call x1, Pallas kernels: 40.2 us -> 35.2 us  [gather_and_cut(): pl.pallas_call(functools.partial(gather_kernel, owners, amps), in_specs=[...]
    pallas_call x2 -> x1, Pallas kernels: 17.1 us -> 15.2 us  [filter_strip(): pl.pallas_call(functools.partial(filter_kernel, columns), grid=(columns /...]
    squeeze x2 -> x0, local copies, waits for them, and re-layouts: 0.9 us -> none  [the longest x1 0.9 us: per_device(): tile_offset[ccd_id, amp_id, :, 1]]
where the time goes in v3:
time: 50.5 us; the launch traced here: 50.4 us
  Pallas kernels  50.4 us (100%)
    pallas_call x1, Pallas kernels, gather_and_cut(): pl.pallas_call(functools.partial(gather_kernel, owners, amps), in_specs=[...  35.2 us
    pallas_call x1, Pallas kernels, filter_strip(): pl.pallas_call(functools.partial(filter_kernel, columns), grid=(columns /...  15.2 us

profile of v3, /device:TPU:0, one launch (start us, length us, event | category | flops | bytes accessed | tf_op | source)
XLA Modules:
  0.0 50.4 jit_solution(5259893961396235528)
XLA Ops:
  0.0 35.2 %shard_map.100 = (bf16[128,4224]{1,0:T(8,128)(2,1)}, bf16[16,4224]{1,0:T(8,128)(2,1)}, bf16[16,4224]{1,0:T(8,128)(2,1)}, bf16[3,128,1792]{2,1,0:T(8,128)(2,1)}, bf16[3,32,256]{2,1,0:T(8,128)(2,1)}) custom-call(s32[8,4,1,32]{3,2,1,0:T(1,128)} %bitcast.7, s32[8,4,32]{2,1,0:T(4,128)} %patch_hbm.1, s32[8,4,2,32]{3,2,1,0:T(2,128)} %bitcast.6, ...), custom_call_target="tpu_custom_call" | custom-call | flops 1073741824 | bytes 6291456 | tf_op jit(solution)/shard_map/pallas_call | solution.py:343
  35.2 15.2 %shard_map.101 = f32[128,4096]{1,0:T(8,128)} custom-call(bf16[128,4224]{1,0:T(8,128)(2,1)} %get-tuple-element.10.template_ref, bf16[16,4224]{1,0:T(8,128)(2,1)} %get-tuple-element.11.top_ref, bf16[16,4224]{1,0:T(8,128)(2,1)} %get-tuple-element.12.low_ref, bf16[256,1792]{1,0:T(8,128)(2,1)} %constant.8.clone.across_ref, ...), custom_call_target="tpu_custom_call" | custom-call | flops 9395240960 | bytes 8388608 | tf_op jit(solution)/shard_map/pallas_call | solution.py:453

commit v4 on v3

--- a/solution.py
+++ b/solution.py
@@ -91,11 +91,17 @@
     down_hbm,
     rim_down_hbm,
     pack_hbm,
+    across_hbm,
+    science_hbm,
+    out_hbm,
     template_ref,
-    top_ref,
-    low_ref,
     weight_ref,
     rim_weight_ref,
+    across_ref,
+    science_ref,
+    result,
+    spread,
+    rim_spread,
     owner_ref,
     patch_ref,
     offset_ref,
@@ -109,6 +115,7 @@
     top_land,
     low_land,
     local_sem,
+    out_sem,
     direct_send,
     direct_recv,
     relay_send,
@@ -156,6 +163,8 @@
                 (owner_hbm.at[mine, amp], owner_ref),
                 (patch_hbm.at[mine], patch_ref),
                 (offset_hbm.at[mine, amp], offset_ref),
+                (across_hbm, across_ref),
+                (science_hbm.at[0], science_ref),
             )
         )
     ]
@@ -322,36 +331,76 @@
     rest = rim_copies(1, pl.ds(early, (tiles + 1) * TS - early))
     for copy in rest:
         copy.start()
+    def receive(copies, where):
+        for copy in copies:
+            copy.wait()
+        blank = jnp.zeros((RIM, where.stop - where.start), jnp.bfloat16)
+        top_land[:, where] = jnp.where(amp > 0, top_land[:, where], blank)
+        low_land[:, where] = jnp.where(amp < amps - 1, low_land[:, where], blank)
+
+    receive(rims, slice(0, early))
+    columns = science_ref.shape[1]
+    width = spread.shape[1]
+
+    def result_copy(i):
+        where = pl.ds(pl.multiple_of(i * width, width), width)
+        return pltpu.make_async_copy(
+            result.at[:, where], out_hbm.at[0, :, where], out_sem.at[i]
+        )
+
+    def chunk(i, carried):
+        @pl.when(i == 1)
+        def _():
+            receive(rest, slice(early, (tiles + 1) * TS))
+
+        filter_chunk(
+            columns,
+            i * width,
+            template_ref,
+            top_land,
+            low_land,
+            across_ref,
+            weight_ref,
+            rim_weight_ref,
+            science_ref,
+            result,
+            spread,
+            rim_spread,
+        )
+        result_copy(i).start()
+        return carried
+
+    lax.fori_loop(0, columns // width, chunk, 0)
     own.wait_send()
     for copy in sent:
         copy.wait_send()
-    for copy in rims + rest:
-        copy.wait()
-    top_ref[...] = jnp.where(amp > 0, top_land[...], jnp.zeros_like(top_land))
-    low_ref[...] = jnp.where(amp < amps - 1, low_land[...], jnp.zeros_like(low_land))
-
-
-def gather_and_cut(owner, patch, offset, coeffs, patches, down, rim_down, pack):
+    for i in range(columns // width):
+        result_copy(i).wait()
+
+
+def gather_and_cut(owner, patch, offset, coeffs, patches, down, rim_down, pack, across, science, chunk_width):
     owners, amps = lax.axis_size("ccd"), lax.axis_size("amp")
     tiles = patch.shape[2]
     count, rows, lanes = down.shape
     width = (tiles + 1) * TS
     rim_lanes = -(-count * RIM // TS) * TS
-    vmem = pl.BlockSpec(memory_space=pltpu.VMEM)
+    strip = science.shape[1:]
     chips = owners // 2
     dma = pltpu.SemaphoreType.DMA
     return pl.pallas_call(
         functools.partial(gather_kernel, owners, amps),
-        in_specs=[pl.BlockSpec(memory_space=pl.ANY)] * 8,
-        out_specs=[vmem] * 5,
-        out_shape=[
-            jax.ShapeDtypeStruct((rows, width), jnp.bfloat16),
-            jax.ShapeDtypeStruct((RIM, width), jnp.bfloat16),
-            jax.ShapeDtypeStruct((RIM, width), jnp.bfloat16),
-            jax.ShapeDtypeStruct((3, rows, count * TS), jnp.bfloat16),
-            jax.ShapeDtypeStruct((3, 2 * RIM, rim_lanes), jnp.bfloat16),
-        ],
+        in_specs=[pl.BlockSpec(memory_space=pl.ANY)] * 10,
+        out_specs=pl.BlockSpec(memory_space=pl.ANY),
+        out_shape=jax.ShapeDtypeStruct(science.shape, jnp.float32),
         scratch_shapes=[
+            pltpu.VMEM((rows, width), jnp.bfloat16),
+            pltpu.VMEM((3, rows, count * TS), jnp.bfloat16),
+            pltpu.VMEM((3, 2 * RIM, rim_lanes), jnp.bfloat16),
+            pltpu.VMEM(across.shape, jnp.bfloat16),
+            pltpu.VMEM(strip, jnp.float32),
+            pltpu.VMEM(strip, jnp.float32),
+            pltpu.VMEM((count * TS, chunk_width), jnp.bfloat16),
+            pltpu.VMEM((2, rim_lanes, chunk_width), jnp.bfloat16),
             pltpu.SMEM(owner.shape[2:], jnp.int32),
             pltpu.SMEM(patch.shape[1:], jnp.int32),
             pltpu.SMEM(offset.shape[2:], jnp.int32),
@@ -364,7 +413,8 @@
             pltpu.VMEM((3, 2 * RIM, count * TS), jnp.bfloat16),
             pltpu.VMEM((RIM, width), jnp.bfloat16),
             pltpu.VMEM((RIM, width), jnp.bfloat16),
-            dma((8,)),
+            dma((10,)),
+            dma((strip[1] // chunk_width,)),
             dma((chips - 1, 2)),
             dma((chips - 1, 2)),
             dma((2,)),
@@ -380,9 +430,9 @@
             collective_id=0, has_side_effects=True, vmem_limit_bytes=VMEM_BYTES
         ),
         cost_estimate=pl.CostEstimate(
-            flops=tiles * 2 * TS * 8 * TS * TS, bytes_accessed=6 * 2**20, transcendentals=0
+            flops=2 * strip[1] * count * TS * (3 * rows + WINDOW), bytes_accessed=10 * 2**20, transcendentals=0
         ),
-    )(owner, patch, offset, coeffs, patches, down, rim_down, pack)
+    )(owner, patch, offset, coeffs, patches, down, rim_down, pack, across, science)
 
 
 def polynomial(folded, xh):
@@ -390,8 +440,9 @@
     return folded[:rows] + xh * (folded[rows : 2 * rows] + xh * folded[2 * rows :])
 
 
-def filter_kernel(
+def filter_chunk(
     columns,
+    first,
     template_ref,
     top_ref,
     low_ref,
@@ -403,9 +454,9 @@
     spread,
     rim_spread,
 ):
-    rows, width = out_ref.shape
+    rows, width = out_ref.shape[0], spread.shape[1]
     blocks = width // TS
-    first = pl.program_id(0) * width
+    here = pl.ds(pl.multiple_of(first, width), width)
     starts = [pl.multiple_of(first + b * TS, TS) for b in range(blocks)]
     parts = [(template_ref, spread, rows), (top_ref, rim_spread.at[0], RIM)]
     parts.append((low_ref, rim_spread.at[1], RIM))
@@ -435,38 +486,12 @@
     xh = (2.0 * position.astype(jnp.float32) + 1.0) / columns - 1.0
     weights = weight_ref[...].reshape(3 * rows, weight_ref.shape[2])
     folded = jnp.dot(weights, spread[...], preferred_element_type=jnp.float32)
-    out_ref[...] = science_ref[...] - polynomial(folded, xh)
+    out_ref[:, here] = science_ref[:, here] - polynomial(folded, xh)
     for side, begin in enumerate((0, rows - RIM)):
         weights = rim_weight_ref[:, side * RIM : (side + 1) * RIM, :]
         weights = weights.reshape(3 * RIM, rim_weight_ref.shape[2])
         folded = jnp.dot(weights, rim_spread[side], preferred_element_type=jnp.float32)
-        out_ref[begin : begin + RIM, :] -= polynomial(folded, xh)
-
-
-def filter_strip(template, top, low, across, weights, rim_weights, science, width):
-    rows, columns = science.shape
-
-    def whole(array):
-        return pl.BlockSpec(array.shape, lambda i: (0,) * array.ndim)
-
-    constant = (template, top, low, across, weights, rim_weights)
-    return pl.pallas_call(
-        functools.partial(filter_kernel, columns),
-        grid=(columns // width,),
-        in_specs=[whole(x) for x in constant] + [pl.BlockSpec((rows, width), lambda i: (0, i))],
-        out_specs=pl.BlockSpec((rows, width), lambda i: (0, i)),
-        out_shape=jax.ShapeDtypeStruct(science.shape, jnp.float32),
-        scratch_shapes=[
-            pltpu.VMEM((weights.shape[2], width), jnp.bfloat16),
-            pltpu.VMEM((2, rim_weights.shape[2], width), jnp.bfloat16),
-        ],
-        compiler_params=pltpu.CompilerParams(vmem_limit_bytes=VMEM_BYTES),
-        cost_estimate=pl.CostEstimate(
-            flops=2 * columns * weights.shape[2] * (3 * rows + WINDOW),
-            bytes_accessed=8 * rows * columns + 4 * 2**20,
-            transcendentals=0,
-        ),
-    )(*constant, science)
+        out_ref[begin : begin + RIM, here] -= polynomial(folded, xh)
 
 
 def per_device(science, patches, coeffs, tile_owner, tile_patch, tile_offset):
@@ -479,7 +504,7 @@
     top_lags = (rim_row[None, :] - RIM) - rim_row[:, None]
     low_lags = (rim_row[None, :] + RIM) - rim_row[:, None]
     rim_down = down_factors(np.concatenate([top_lags, low_lags], axis=0), TS)
-    template, top, low, weights, rim_weights = gather_and_cut(
+    return gather_and_cut(
         jnp.transpose(tile_owner, (0, 1, 3, 2)),
         tile_patch,
         jnp.transpose(tile_offset, (0, 1, 3, 2)),
@@ -488,10 +513,10 @@
         jnp.asarray(down),
         jnp.asarray(rim_down),
         jnp.asarray(lane_packing()),
+        across,
+        science,
+        8 * TS,
     )
-    return filter_strip(
-        template, top, low, across, weights, rim_weights, science[0], 8 * TS
-    )[None]
 
 
 def solution(mesh):

time: 50.5 us -> 47.9 us (0.949)
  Pallas kernels: 50.4 us -> 44.7 us
  local copies, waits for them, and re-layouts: 0 us -> 3.11 us
    pallas_call x1 -> x0, Pallas kernels: 15.2 us -> none  [filter_strip(): pl.pallas_call(functools.partial(filter_kernel, columns), grid=(columns /...]
    pallas_call x1, Pallas kernels: 35.2 us -> 44.7 us  [gather_and_cut(): pl.pallas_call(functools.partial(gather_kernel, owners, amps), in_specs=[...]
    unnamed x0 -> x1, local copies, waits for them, and re-layouts: none -> 3.11 us
where the time goes in v4:
time: 47.9 us; the launch traced here: 47.8 us
  Pallas kernels  44.7 us (93%)
  local copies, waits for them, and re-layouts  3.11 us (6%)
    pallas_call x1, Pallas kernels, gather_and_cut(): pl.pallas_call(functools.partial(gather_kernel, owners, amps), in_specs=[...  44.7 us
    unnamed x1, local copies, waits for them, and re-layouts  3.11 us

profile of v4, /device:TPU:0, one launch (start us, length us, event | category | flops | bytes accessed | tf_op | source)
XLA Modules:
  0.0 47.8 jit_solution(1995442656952552687)
XLA Ops:
  0.0 44.7 %shard_map.100 = f32[1,128,4096]{2,1,0:T(8,128)} custom-call(s32[8,4,1,32]{3,2,1,0:T(1,128)} %bitcast.4, s32[8,4,32]{2,1,0:T(4,128)} %patch_hbm.1, s32[8,4,2,32]{3,2,1,0:T(2,128)} %bitcast.3, f32[6,1,40]{2,1,0:T(1,128)} %bitcast.5, f32[1,1,4,256,256]{4,3,2,1,0:T(8,128)} %patches_hbm.1, bf16[14,128,128]{2,1,0:T(8,128)(2,1)} %constant.9.clone.down_hbm, ...), custom_call_target="tpu_custom_call" | custom-call | flops 9395240960 | bytes 10485760 | tf_op jit(solution)/shard_map/pallas_call | solution.py:390
  44.7 3.1 %copy.12 = f32[1,128,4096]{2,1,0:T(8,128)} copy(f32[1,128,4096]{2,1,0:T(8,128)} %shard_map.100) | data formatting | bytes 4194304

commit v5 on v4

--- a/solution.py
+++ b/solution.py
@@ -92,13 +92,11 @@
     rim_down_hbm,
     pack_hbm,
     across_hbm,
-    science_hbm,
     out_hbm,
     template_ref,
     weight_ref,
     rim_weight_ref,
     across_ref,
-    science_ref,
     result,
     spread,
     rim_spread,
@@ -164,7 +162,6 @@
                 (patch_hbm.at[mine], patch_ref),
                 (offset_hbm.at[mine, amp], offset_ref),
                 (across_hbm, across_ref),
-                (science_hbm.at[0], science_ref),
             )
         )
     ]
@@ -339,7 +336,7 @@
         low_land[:, where] = jnp.where(amp < amps - 1, low_land[:, where], blank)
 
     receive(rims, slice(0, early))
-    columns = science_ref.shape[1]
+    columns = result.shape[1]
     width = spread.shape[1]
 
     def result_copy(i):
@@ -362,7 +359,6 @@
             across_ref,
             weight_ref,
             rim_weight_ref,
-            science_ref,
             result,
             spread,
             rim_spread,
@@ -389,7 +385,7 @@
     dma = pltpu.SemaphoreType.DMA
     return pl.pallas_call(
         functools.partial(gather_kernel, owners, amps),
-        in_specs=[pl.BlockSpec(memory_space=pl.ANY)] * 10,
+        in_specs=[pl.BlockSpec(memory_space=pl.ANY)] * 9,
         out_specs=pl.BlockSpec(memory_space=pl.ANY),
         out_shape=jax.ShapeDtypeStruct(science.shape, jnp.float32),
         scratch_shapes=[
@@ -397,7 +393,6 @@
             pltpu.VMEM((3, rows, count * TS), jnp.bfloat16),
             pltpu.VMEM((3, 2 * RIM, rim_lanes), jnp.bfloat16),
             pltpu.VMEM(across.shape, jnp.bfloat16),
-            pltpu.VMEM(strip, jnp.float32),
             pltpu.VMEM(strip, jnp.float32),
             pltpu.VMEM((count * TS, chunk_width), jnp.bfloat16),
             pltpu.VMEM((2, rim_lanes, chunk_width), jnp.bfloat16),
@@ -432,7 +427,7 @@
         cost_estimate=pl.CostEstimate(
             flops=2 * strip[1] * count * TS * (3 * rows + WINDOW), bytes_accessed=10 * 2**20, transcendentals=0
         ),
-    )(owner, patch, offset, coeffs, patches, down, rim_down, pack, across, science)
+    )(owner, patch, offset, coeffs, patches, down, rim_down, pack, across)
 
 
 def polynomial(folded, xh):
@@ -449,7 +444,6 @@
     across_ref,
     weight_ref,
     rim_weight_ref,
-    science_ref,
     out_ref,
     spread,
     rim_spread,
@@ -486,12 +480,12 @@
     xh = (2.0 * position.astype(jnp.float32) + 1.0) / columns - 1.0
     weights = weight_ref[...].reshape(3 * rows, weight_ref.shape[2])
     folded = jnp.dot(weights, spread[...], preferred_element_type=jnp.float32)
-    out_ref[:, here] = science_ref[:, here] - polynomial(folded, xh)
+    out_ref[:, here] = polynomial(folded, xh)
     for side, begin in enumerate((0, rows - RIM)):
         weights = rim_weight_ref[:, side * RIM : (side + 1) * RIM, :]
         weights = weights.reshape(3 * RIM, rim_weight_ref.shape[2])
         folded = jnp.dot(weights, rim_spread[side], preferred_element_type=jnp.float32)
-        out_ref[begin : begin + RIM, here] -= polynomial(folded, xh)
+        out_ref[begin : begin + RIM, here] += polynomial(folded, xh)
 
 
 def per_device(science, patches, coeffs, tile_owner, tile_patch, tile_offset):
@@ -504,7 +498,7 @@
     top_lags = (rim_row[None, :] - RIM) - rim_row[:, None]
     low_lags = (rim_row[None, :] + RIM) - rim_row[:, None]
     rim_down = down_factors(np.concatenate([top_lags, low_lags], axis=0), TS)
-    return gather_and_cut(
+    psf_model = gather_and_cut(
         jnp.transpose(tile_owner, (0, 1, 3, 2)),
         tile_patch,
         jnp.transpose(tile_offset, (0, 1, 3, 2)),
@@ -517,6 +511,7 @@
         science,
         8 * TS,
     )
+    return science - psf_model
 
 
 def solution(mesh):

time: 47.9 us -> 48.7 us (1.017)
  other arithmetic: 0 us -> 3.17 us
  local copies, waits for them, and re-layouts: 3.11 us -> 0.01 us
  Pallas kernels: 44.7 us -> 45.4 us
    sub x0 -> x1, other arithmetic: none -> 3.17 us  [per_device(): return science - psf_model]
    unnamed x1 -> x2, local copies, waits for them, and re-layouts: 3.11 us -> 0.01 us
    pallas_call x1, Pallas kernels: 44.7 us -> 45.4 us  [gather_and_cut(): pl.pallas_call(functools.partial(gather_kernel, owners, amps), in_specs=[...]
where the time goes in v5:
time: 48.7 us; the launch traced here: 48.5 us
  Pallas kernels  45.4 us (93%)
  other arithmetic  3.17 us (7%)
    pallas_call x1, Pallas kernels, gather_and_cut(): pl.pallas_call(functools.partial(gather_kernel, owners, amps), in_specs=[...  45.4 us
    sub x1, other arithmetic, per_device(): return science - psf_model  3.17 us

profile of v5, /device:TPU:0, one launch (start us, length us, event | category | flops | bytes accessed | tf_op | source)
XLA Modules:
  0.0 48.5 jit_solution(17596759314889454189)
XLA Ops:
  0.0 0.0 copy-start
  0.0 45.4 %shard_map.100 = f32[1,128,4096]{2,1,0:T(8,128)} custom-call(s32[8,4,1,32]{3,2,1,0:T(1,128)} %bitcast.4, s32[8,4,32]{2,1,0:T(4,128)} %patch_hbm.1, s32[8,4,2,32]{3,2,1,0:T(2,128)} %bitcast.3, f32[6,1,40]{2,1,0:T(1,128)} %bitcast.5, f32[1,1,4,256,256]{4,3,2,1,0:T(8,128)} %patches_hbm.1, bf16[14,128,128]{2,1,0:T(8,128)(2,1)} %constant.9.clone.down_hbm, ...), custom_call_target="tpu_custom_call" | custom-call | flops 9395240960 | bytes 10485760 | tf_op jit(solution)/shard_map/pallas_call | solution.py:386
  45.4 0.0 copy-done
  45.4 3.2 %sub.3 = f32[1,128,4096]{2,1,0:T(8,128)} subtract(f32[1,128,4096]{2,1,0:T(8,128)S(1)} %copy-done, f32[1,128,4096]{2,1,0:T(8,128)} %shard_map.100) | non-fusion elementwise | flops 524288 | bytes 6291456 | tf_op jit(solution)/shard_map/sub | solution.py:514
Async XLA Ops:
  0.0 45.4 %copy-start = (f32[1,128,4096]{2,1,0:T(8,128)S(1)}, f32[1,128,4096]{2,1,0:T(8,128)}, u32[]{:S(2)}) copy-start(f32[1,128,4096]{2,1,0:T(8,128)} %param.10) | copy-start | bytes 6291460
